TPU v7x, 128 devices: a whole 4x4x4 slice. The times are simulated.
128 devices in a mesh: dp: 4 (over x), tp: 32 (over z, y, core).
Axes of the slice: x: 4, y: 4, z: 4, core: 2. Of those that a mesh axis runs over, the one named last changes fastest.
Arguments:
- hidden: bfloat16 [8192, 14784], P(('dp', 'tp')), may hold values from -6 to 6
- draft_row_client: int32 [8192], P(('dp', 'tp')), may hold values from 0 to 255, as said below
- client_rank_bin: int32 [256], replicated, may hold values from 8 to 256, as said below
- client_device: int32 [256], replicated, may hold values from 0 to 127, as said below
- down_weight: bfloat16 [14784, 8192], P('tp'), may hold values from -0.046875 to 0.046875
- packed_down_factors: bfloat16 [14784, 40960], P(None, ('dp', 'tp')), may hold values from -0.046875 to 0.046875
- packed_up_factors: bfloat16 [40960, 8192], P(('dp', 'tp')), may hold values from -0.75 to 0.75
Outputs:
- projected: bfloat16 [8192, 8192], P(('dp', 'tp'))
Inputs may be any that keep to these rules, and one draw needn't show every extreme that they name: `client_device`: each device holds exactly two tenants. `client_rank_bin`: ranks are powers of two; the two tenants of one device have ranks summing to at most 320, and some device's sum is exactly 320; a device's adapters are packed from its first column in increasing tenant order. `draft_row_client`: of the rows of one device, at most 24 belong to tenants whose device lies in any one dp group; of all rows on the devices of one tp index whose tenants lie in one dp group, at most 3 belong to the tenants of any one device of that group.
All inputs are finite; a program needn't handle non-finite values.
Results may differ from a plain program's by a relative error of at most 0.0065.
Values may be sent and summed in bfloat16 or wider, within the bound.
A program may use at most 448 MiB of HBM per device.

v0:
```python
import jax
import jax.numpy as jnp
from jax import lax
from jax.sharding import PartitionSpec as P

adapter_scale_fn = 4.0


def adapter_tables(client_rank_bin, client_device):
    client_indices = jnp.arange(client_rank_bin.shape[0], dtype=jnp.int32)
    earlier = (client_device[:, None] == client_device[None, :]) & (
        client_indices[None, :] < client_indices[:, None]
    )
    column_offset = jnp.sum(jnp.where(earlier, client_rank_bin[None, :], 0), axis=1)
    adapter_scale = adapter_scale_fn / jnp.sqrt(client_rank_bin.astype(jnp.float32))
    return (column_offset, adapter_scale)


def lookup(client_indices, table_values):
    matches = client_indices[:, None] == jnp.arange(table_values.shape[0], dtype=jnp.int32)[None, :]
    return jnp.sum(
        jnp.where(matches, table_values[None, :], jnp.zeros((), table_values.dtype)), axis=1
    )


def bucket_matrix(bucket_id, occupied, buckets, capacity):
    matches = (bucket_id[:, None] == jnp.arange(buckets, dtype=jnp.int32)[None, :]) & occupied[
        :, None
    ]
    rank_in = jnp.cumsum(matches.astype(jnp.int32), axis=0) - 1
    within = jnp.sum(jnp.where(matches, rank_in, 0), axis=1)
    target = jnp.where(occupied, bucket_id * capacity + within, -1)
    return jnp.arange(buckets * capacity, dtype=jnp.int32)[:, None] == target[None, :]


def adapter_row_block(
    row_span,
    client_indices,
    column_offset,
    client_rank_bin,
    adapter_scale,
    packed_down_factors,
    packed_up_factors,
):
    projected = jnp.dot(row_span, packed_down_factors, preferred_element_type=jnp.float32)
    col_start = lookup(client_indices, column_offset)
    col_count = lookup(client_indices, client_rank_bin)
    row_gain = lookup(client_indices, adapter_scale)
    column_span = jnp.arange(packed_down_factors.shape[1], dtype=jnp.int32)[None, :]
    in_range = (column_span >= col_start[:, None]) & (
        column_span < (col_start + col_count)[:, None]
    )
    rank_space = (jnp.where(in_range, projected, 0.0) * row_gain[:, None]).astype(jnp.bfloat16)
    return jnp.dot(rank_space, packed_up_factors, preferred_element_type=jnp.float32)


def local(
    hidden,
    draft_row_client,
    client_rank_bin,
    client_device,
    down_weight,
    packed_down_factors,
    packed_up_factors,
):
    dp_count = lax.axis_size("dp")
    tp_count = lax.axis_size("tp")
    rows_home = hidden.shape[0]
    width = down_weight.shape[1]
    group_cap = 3 * rows_home // 8
    owner_cap = max(2, (dp_count * group_cap + tp_count - 1) // tp_count)
    slots = dp_count * group_cap
    column_offset, adapter_scale = adapter_tables(client_rank_bin, client_device)
    home_device = lookup(draft_row_client, client_device)
    home_pick = bucket_matrix(
        home_device // tp_count, jnp.ones((rows_home,), bool), dp_count, group_cap
    )
    packed = jnp.dot(
        home_pick.astype(jnp.bfloat16), hidden, preferred_element_type=jnp.float32
    ).astype(jnp.bfloat16)
    packed_tenant = jnp.sum(jnp.where(home_pick, draft_row_client[None, :] + 1, 0), axis=1) - 1
    group_rows, group_tenant = (
        lax.all_to_all(
            packed.reshape(dp_count, group_cap, -1), "dp", split_axis=0, concat_axis=0, tiled=True
        ),
        lax.all_to_all(
            packed_tenant.reshape(dp_count, group_cap),
            "dp",
            split_axis=0,
            concat_axis=0,
            tiled=True,
        ),
    )
    group_rows = group_rows.reshape(slots, -1)
    group_tenant = group_tenant.reshape(slots)
    occupied = group_tenant >= 0
    group_device = lookup(group_tenant, client_device)
    owner_pick = bucket_matrix(group_device % tp_count, occupied, tp_count, owner_cap)
    owner_rows = jnp.dot(
        owner_pick.astype(jnp.bfloat16), group_rows, preferred_element_type=jnp.float32
    ).astype(jnp.bfloat16)
    owner_tenant = jnp.sum(jnp.where(owner_pick, group_tenant[None, :] + 1, 0), axis=1) - 1
    owner_spot = jnp.sum(
        jnp.where(owner_pick, jnp.arange(slots, dtype=jnp.int32)[None, :], 0), axis=1
    )
    got_rows, got_tenant, got_spot = (
        lax.all_to_all(
            owner_rows.reshape(tp_count, owner_cap, -1),
            "tp",
            split_axis=0,
            concat_axis=0,
            tiled=True,
        ),
        lax.all_to_all(
            owner_tenant.reshape(tp_count, owner_cap), "tp", split_axis=0, concat_axis=0, tiled=True
        ),
        lax.all_to_all(
            owner_spot.reshape(tp_count, owner_cap), "tp", split_axis=0, concat_axis=0, tiled=True
        ),
    )
    adapter_out = adapter_row_block(
        got_rows.reshape(tp_count * owner_cap, -1),
        got_tenant.reshape(-1),
        column_offset,
        client_rank_bin,
        adapter_scale,
        packed_down_factors,
        packed_up_factors,
    )
    features = lax.all_to_all(
        group_rows.reshape(slots, tp_count, -1), "tp", split_axis=1, concat_axis=0, tiled=True
    ).reshape(tp_count * slots, -1)
    arrived = lax.all_to_all(
        adapter_out.reshape(tp_count, owner_cap, width).astype(jnp.bfloat16),
        "tp",
        split_axis=0,
        concat_axis=0,
        tiled=True,
    ).astype(jnp.float32)
    mixed = lax.psum_scatter(
        jnp.dot(features, down_weight, preferred_element_type=jnp.float32),
        "tp",
        scatter_dimension=0,
        tiled=True,
    ) + jnp.dot(
        owner_pick.astype(jnp.float32).T,
        arrived.reshape(tp_count * owner_cap, width),
        precision=lax.Precision.HIGHEST,
    )
    finished = mixed.astype(jnp.bfloat16)
    home_rows = lax.all_to_all(
        finished.reshape(dp_count, group_cap, width), "dp", split_axis=0, concat_axis=0, tiled=True
    ).reshape(slots, width)
    return jnp.dot(
        home_pick.astype(jnp.bfloat16).T, home_rows, preferred_element_type=jnp.float32
    ).astype(jnp.bfloat16)


def solution(mesh):
    placed = (
        P(("dp", "tp"), None),
        P(("dp", "tp")),
        P(),
        P(),
        P("tp", None),
        P(None, ("dp", "tp")),
        P(("dp", "tp"), None),
    )
    return jax.shard_map(
        local, mesh=mesh, in_specs=placed, out_specs=P(("dp", "tp"), None), check_vma=False
    )
```

profile of v0, /device:TPU:0, one launch (start us, length us, event | category | flops | bytes accessed | tf_op | source)
XLA Modules:
  0.0 585.0 jit_solution(13557641320100263617)
XLA Ops:
  6.5 1.0 select_reduce_fusion.5
  8.6 1.0 convolution_convert_fusion.1
  9.6 38.6 %all_to_all.47 = bf16[4,24,14784]{2,1,0:T(8,128)(2,1)S(1)} all-to-all(bf16[4,24,14784]{2,1,0:T(8,128)(2,1)S(1)} %bitcast.21), channel_id=1, replica_groups=mesh['dp'=4,'tp'=32] {'dp'}, dimensions={0} | all-to-all | bytes 5677056 | tf_op jit(solution)/shard_map/all_to_all | solution.py:83
  48.2 7.8 %reshape_reshape.3 = bf16[96,32,462]{2,1,0:T(8,128)(2,1)} reshape(bf16[4,24,14784]{2,1,0:T(8,128)(2,1)S(1)} %all_to_all.47) | data formatting | bytes 5677056 | tf_op jit(solution)/shard_map/reshape;reshape | solution.py:131
  56.0 3.6 copy.12
  59.7 48.0 %all_to_all.48 = bf16[96,32,462]{2,0,1:T(8,128)(2,1)} all-to-all(bf16[96,32,462]{2,0,1:T(8,128)(2,1)S(1)} %copy.12), channel_id=1, replica_groups=mesh['dp'=4,'tp'=32] {'tp'}, dimensions={1} | all-to-all | bytes 5677056 | tf_op jit(solution)/shard_map/all_to_all | solution.py:130
  107.7 43.0 %fusion.19 = f32[3072,8192]{1,0:T(8,128)} fusion(bf16[3072,462]{1,0:T(8,128)(2,1)} %bitcast.24, bf16[462,8192]{1,0:T(8,128)(2,1)} %param.11), kind=kOutput, calls=%fused_computation.59 | convolution fusion | flops 23253221376 | bytes 111071232 | tf_op jit(solution)/shard_map/dot_general | solution.py:141
  150.9 7.6 %all_to_all.49 = s32[4,1,24]{2,1,0:T(1,128)S(1)} all-to-all(s32[4,1,24]{2,1,0:T(1,128)S(1)} %bitcast.25), channel_id=1, replica_groups=mesh['dp'=4,'tp'=32] {'dp'}, dimensions={0} | all-to-all | bytes 768 | tf_op jit(solution)/shard_map/all_to_all | solution.py:86
  160.7 0.7 sub.30
  161.4 4.0 all-to-all-start.3
  165.4 2.6 convolution_convert_fusion
  168.1 5.5 reshape.174
  173.5 7.6 %all-to-all-start.4 = ((bf16[32,3,14784]{2,1,0:T(4,128)(2,1)}), bf16[32,3,14784]{2,1,0:T(4,128)(2,1)}, u32[]{:S(2)}, u32[]{:S(2)}) async-start(bf16[32,3,14784]{2,1,0:T(4,128)(2,1)} %reshape.174), calls=%async_computation.5 | async-start | bytes 7602176 | tf_op jit(solution)/shard_map/all_to_all | solution.py:107
  181.3 0.7 reduce.7
  182.5 47.7 %all-to-all-done.4 = bf16[32,3,14784]{2,1,0:T(4,128)(2,1)} async-done(((bf16[32,3,14784]{2,1,0:T(4,128)(2,1)}), bf16[32,3,14784]{2,1,0:T(4,128)(2,1)}, u32[]{:S(2)}, u32[]{:S(2)}) %all-to-all-start.4) | async-done | bytes 2838560 | tf_op jit(solution)/shard_map/all_to_all | solution.py:107
  230.2 4.6 reshape.175
  234.8 15.7 %convolution_convert_fusion.2 = bf16[96,8192]{1,0:T(8,128)(2,1)} fusion(bf16[320,8192]{1,0:T(8,128)(2,1)} %param.13, bf16[96,14784]{1,0:T(8,128)(2,1)S(1)} %reshape.175, bf16[14784,320]{0,1:T(8,128)(2,1)} %param.12, f32[96]{0:T(128)S(1)} %select_reduce_fusion.1, s32[96]{0:T(128)S(1)} %add.93, s32[96]{0:T(128)S(1)} %get-tuple-element.6), kind=kOutput, calls=%fused_computation.4 | convolution fusion | flops 1412616192 | bytes 19117184 | tf_op jit(solution)/shard_map/dot_general | solution.py:54
  250.5 2.9 convert_element_type.42
  253.4 33.4 %all_to_all.50 = bf16[32,3,8192]{2,1,0:T(4,128)(2,1)} all-to-all(bf16[32,3,8192]{2,1,0:T(4,128)(2,1)S(1)} %convert_element_type.42), channel_id=1, replica_groups=mesh['dp'=4,'tp'=32] {'tp'}, dimensions={0} | all-to-all | bytes 3145728 | tf_op jit(solution)/shard_map/all_to_all | solution.py:133
  286.8 3.2 reshape.176
  290.0 259.2 %reduce-scatter.2.cloned.1.call-done = f32[96,8192]{1,0:T(8,128)} async-done(((f32[3072,8192]{1,0:T(8,128)}), f32[96,8192]{1,0:T(8,128)}) %reduce-scatter.2.cloned.1.call-update) | async-done | bytes 3145744 | tf_op jit(solution)/shard_map/reduce_scatter | solution.py:140
  549.2 2.5 fusion
  551.7 24.9 %all_to_all.51 = bf16[4,24,8192]{2,1,0:T(8,128)(2,1)S(1)} all-to-all(bf16[4,24,8192]{2,1,0:T(8,128)(2,1)S(1)} %bitcast.23), channel_id=1, replica_groups=mesh['dp'=4,'tp'=32] {'dp'}, dimensions={0} | all-to-all | bytes 3145728 | tf_op jit(solution)/shard_map/all_to_all | solution.py:151
  576.7 1.5 convolution_convert_fusion.3
  (37 shorter events, 4.0 us)
Async XLA Ops:
  6.5 2.1 copy-start
  6.5 542.7 %reduce-scatter.2.cloned.1.call-start = ((), (), s32[]{:S(2)}) async-start(), calls=%async_computation.8 | async-start | bytes 103809024 | tf_op jit(solution)/shard_map/reduce_scatter | solution.py:140
  150.7 9.2 %copy-start.2 = (s32[256]{0:T(256)S(1)}, s32[256]{0:T(256)}, u32[]{:S(2)}) copy-start(s32[256]{0:T(256)} %param.10) | copy-start | bytes 3076
  161.4 12.1 %all-to-all-start.3 = ((s32[32,1,3]{2,1,0:T(1,128)}), s32[32,1,3]{2,1,0:T(1,128)S(1)}, u32[]{:S(2)}, u32[]{:S(2)}) async-start(s32[32,1,3]{2,1,0:T(1,128)} %bitcast.5), calls=%async_computation.4 | async-start | bytes 32768 | tf_op jit(solution)/shard_map/all_to_all | solution.py:114
  173.5 7.6 %copy-start.3 = (s32[256]{0:T(256)S(1)}, s32[256]{0:T(256)}, u32[]{:S(2)}) copy-start(s32[256]{0:T(256)} %param.9) | copy-start | bytes 3076
  173.5 56.7 %all-to-all-start.4 = ((bf16[32,3,14784]{2,1,0:T(4,128)(2,1)}), bf16[32,3,14784]{2,1,0:T(4,128)(2,1)}, u32[]{:S(2)}, u32[]{:S(2)}) async-start(bf16[32,3,14784]{2,1,0:T(4,128)(2,1)} %reshape.174), calls=%async_computation.5 | async-start | bytes 7602176 | tf_op jit(solution)/shard_map/all_to_all | solution.py:107
  551.7 26.4 %copy-start.1 = (bf16[64,14784]{1,0:T(8,128)(2,1)S(1)}, bf16[64,14784]{1,0:T(8,128)(2,1)}, u32[]{:S(2)}) copy-start(bf16[64,14784]{1,0:T(8,128)(2,1)} %param.7) | copy-start | bytes 5677060
Sparse Core Ops, SparseCore 0:
  150.8 398.3 reduce-scatter.1
where the time goes:
time: 586 us; the launch traced here: 585 us
  waiting for transfers between devices  307 us (52%)
  blocking collectives  153 us (26%)
  matrix products  66.3 us (11%)
  local copies, waits for them, and re-layouts  29.2 us (5%)
  between operations  13.6 us (2%)
  starting transfers between devices  11.6 us (2%)
    reduce_scatter x1, waiting for transfers between devices, local(): lax.psum_scatter(jnp.dot(features, down_weight, preferred_element_type=jn...  259 us
    all_to_all x1, blocking collectives, local(): lax.all_to_all(group_rows.reshape(slots, tp_count, -1), 'tp', split_axis=...  48 us
    all_to_all x1, waiting for transfers between devices, local(): lax.all_to_all(owner_rows.reshape(tp_count, owner_cap, -1), 'tp', split_a...  47.7 us
    dot_general x1, matrix products, local(): jnp.dot(features, down_weight, preferred_element_type=jnp.float32)  43 us
    all_to_all x1, blocking collectives, local(): lax.all_to_all(packed.reshape(dp_count, group_cap, -1), 'dp', split_axis=...  38.6 us
    all_to_all x1, blocking collectives, local(): lax.all_to_all(adapter_out.reshape(tp_count, owner_cap, width).astype(jnp...  33.4 us
    all_to_all x1, blocking collectives, local(): lax.all_to_all(finished.reshape(dp_count, group_cap, width), 'dp', split_...  24.9 us
    dot_general x1, matrix products, adapter_row_block(): jnp.dot(rank_space, packed_up_factors, preferred_element_type=jnp.float32)  15.7 us
  transfers between devices with their start and end apart: 3, of which 2 were waited for; matrix products, arithmetic and copies ran while one was open for 7% of the time, Pallas kernels for 0%

commit v1 on v0

--- a/solution.py
+++ b/solution.py
@@ -70,6 +70,25 @@
     group_cap = 3 * rows_home // 8
     owner_cap = max(2, (dp_count * group_cap + tp_count - 1) // tp_count)
     slots = dp_count * group_cap
+    chips = tp_count // 2
+    pairs = [[2 * i, 2 * i + 1] for i in range(chips)]
+    plane = [[2 * i + core for i in range(chips)] for core in range(2)]
+    weight = lax.all_gather(down_weight, "tp", axis_index_groups=pairs, tiled=True)
+    features = lax.all_to_all(
+        hidden.reshape(rows_home, chips, -1),
+        "tp",
+        split_axis=1,
+        concat_axis=0,
+        axis_index_groups=plane,
+        tiled=True,
+    ).reshape(chips * rows_home, -1)
+    base = lax.psum_scatter(
+        jnp.dot(features, weight, preferred_element_type=jnp.float32).astype(jnp.bfloat16),
+        "tp",
+        scatter_dimension=0,
+        axis_index_groups=plane,
+        tiled=True,
+    )
     column_offset, adapter_scale = adapter_tables(client_rank_bin, client_device)
     home_device = lookup(draft_row_client, client_device)
     home_pick = bucket_matrix(
@@ -127,33 +146,25 @@
         packed_down_factors,
         packed_up_factors,
     )
-    features = lax.all_to_all(
-        group_rows.reshape(slots, tp_count, -1), "tp", split_axis=1, concat_axis=0, tiled=True
-    ).reshape(tp_count * slots, -1)
     arrived = lax.all_to_all(
         adapter_out.reshape(tp_count, owner_cap, width).astype(jnp.bfloat16),
         "tp",
         split_axis=0,
         concat_axis=0,
         tiled=True,
-    ).astype(jnp.float32)
-    mixed = lax.psum_scatter(
-        jnp.dot(features, down_weight, preferred_element_type=jnp.float32),
-        "tp",
-        scatter_dimension=0,
-        tiled=True,
-    ) + jnp.dot(
-        owner_pick.astype(jnp.float32).T,
+    )
+    group_out = jnp.dot(
+        owner_pick.astype(jnp.bfloat16).T,
         arrived.reshape(tp_count * owner_cap, width),
-        precision=lax.Precision.HIGHEST,
+        preferred_element_type=jnp.float32,
+    ).astype(jnp.bfloat16)
+    home_rows = lax.all_to_all(
+        group_out.reshape(dp_count, group_cap, width), "dp", split_axis=0, concat_axis=0, tiled=True
+    ).reshape(slots, width)
+    adapter = jnp.dot(
+        home_pick.astype(jnp.bfloat16).T, home_rows, preferred_element_type=jnp.float32
     )
-    finished = mixed.astype(jnp.bfloat16)
-    home_rows = lax.all_to_all(
-        finished.reshape(dp_count, group_cap, width), "dp", split_axis=0, concat_axis=0, tiled=True
-    ).reshape(slots, width)
-    return jnp.dot(
-        home_pick.astype(jnp.bfloat16).T, home_rows, preferred_element_type=jnp.float32
-    ).astype(jnp.bfloat16)
+    return (base.astype(jnp.float32) + adapter).astype(jnp.bfloat16)
 
 
 def solution(mesh):

time: 586 us -> 299 us (0.51)
  waiting for transfers between devices: 307 us -> 110 us
  blocking collectives: 153 us -> 57.4 us
  matrix products: 66.3 us -> 46.8 us
  starting transfers between devices: 11.6 us -> 29.4 us
  local copies, waits for them, and re-layouts: 29.2 us -> 37.9 us
    reduce_scatter x1, waiting for transfers between devices: 259 us -> 0.01 us  [local(): lax.psum_scatter(jnp.dot(features, weight, preferred_element_type=jnp.flo...]
    all_to_all x4 -> x1, blocking collectives: 119 us -> 25.1 us  [local(): lax.all_to_all(group_out.reshape(dp_count, group_cap, width), 'dp', split...]
    all_to_all x0 -> x3, waiting for transfers between devices: none -> 33.6 us  [the longest x1 31 us: local(): lax.all_to_all(packed.reshape(dp_count, group_cap, -1), 'dp', split_axis=...]
    dot_general x2, matrix products: 45.5 us -> 26 us  [the longest x1 25.3 us: local(): jnp.dot(features, weight, preferred_element_type=jnp.float32)]
    all_gather x0 -> x1, waiting for transfers between devices: none -> 18.7 us  [local(): lax.all_gather(down_weight, 'tp', axis_index_groups=pairs, tiled=True)]
    all_to_all x0 -> x3, starting transfers between devices: none -> 16.2 us  [the longest x1 8.13 us: local(): lax.all_to_all(hidden.reshape(rows_home, chips, -1), 'tp', split_axis=1,...]
    unnamed x8 -> x11, local copies, waits for them, and re-layouts: 0.02 us -> 14.8 us
    another operation x2 -> x0, local copies, waits for them, and re-layouts: 11.5 us -> none  [local(): group_rows.reshape(slots, tp_count, -1)]
  transfers between devices with their start and end apart: 3 -> 7, of which waited for: 2 -> 5; matrix products, arithmetic and copies ran while one was open for 7% -> 20% of each run, Pallas kernels for 0% -> 0%
where the time goes in v1:
time: 299 us
  waiting for transfers between devices  110 us (37%)
  blocking collectives  57.4 us (19%)
  matrix products  46.8 us (16%)
  local copies, waits for them, and re-layouts  37.9 us (13%)
  starting transfers between devices  29.4 us (10%)
  between operations  13.6 us (5%)
  other arithmetic  3.12 us (1%)
    all_to_all x1, waiting for transfers between devices, local(): lax.all_to_all(owner_rows.reshape(tp_count, owner_cap, -1), 'tp', split_a...  55.6 us
    all_to_all x1, blocking collectives, local(): lax.all_to_all(adapter_out.reshape(tp_count, owner_cap, width).astype(jnp...  32.3 us
    all_to_all x1, waiting for transfers between devices, local(): lax.all_to_all(packed.reshape(dp_count, group_cap, -1), 'dp', split_axis=...  31 us
    dot_general x1, matrix products, local(): jnp.dot(features, weight, preferred_element_type=jnp.float32)  25.3 us
    all_to_all x1, blocking collectives, local(): lax.all_to_all(group_out.reshape(dp_count, group_cap, width), 'dp', split...  25.1 us
    all_gather x1, waiting for transfers between devices, local(): lax.all_gather(down_weight, 'tp', axis_index_groups=pairs, tiled=True)  18.7 us
    unnamed x11, local copies, waits for them, and re-layouts  14.8 us
    dot_general x1, matrix products, adapter_row_block(): jnp.dot(rank_space, packed_up_factors, preferred_element_type=jnp.float32)  12.8 us
  transfers between devices with their start and end apart: 7, of which 5 were waited for; matrix products, arithmetic and copies ran while one was open for 20% of the time, Pallas kernels for 0%

profile of v1, /device:TPU:0, one launch (start us, length us, event | category | flops | bytes accessed | tf_op | source)
XLA Modules:
  0.0 298.5 jit_solution(8723059911654174553)
XLA Ops:
  7.3 5.3 %reshape.173 = bf16[64,16,924]{2,1,0:T(8,128)(2,1)S(1)} reshape(bf16[64,14784]{1,0:T(8,128)(2,1)} %param.7) | data formatting | bytes 3784704 | tf_op jit(solution)/shard_map/reshape | solution.py:78
  12.6 2.5 copy.12
  15.1 8.1 %all-to-all-start = ((bf16[64,16,924]{2,0,1:T(8,128)(2,1)}), bf16[64,16,924]{2,0,1:T(8,128)(2,1)S(1)}, u32[]{:S(2)}, u32[]{:S(2)}) async-start(bf16[64,16,924]{2,0,1:T(8,128)(2,1)} %copy.12), calls=%async_computation | async-start | bytes 4194304 | tf_op jit(solution)/shard_map/all_to_all | solution.py:77
  23.2 18.7 %all-gather.3.cloned.1.call-done = bf16[2,462,8192]{2,1,0:T(8,128)(2,1)} async-done(((bf16[1,462,8192]{2,1,0:T(8,128)(2,1)}), bf16[2,462,8192]{2,1,0:T(8,128)(2,1)}) %all-gather.3.cloned.1.call-update) | async-done | bytes 15138832 | tf_op jit(solution)/shard_map/all_gather | solution.py:76
  41.9 14.1 %reshape.184 = bf16[924,8192]{1,0:T(8,128)(2,1)} reshape(bf16[2,462,8192]{2,1,0:T(8,128)(2,1)} %all-gather.3.cloned.1.call-done) | data formatting | bytes 30277632
  56.0 25.3 %convolution_convert_fusion.2 = bf16[1024,8192]{1,0:T(8,128)(2,1)} fusion(bf16[1024,924]{1,0:T(8,128)(2,1)S(1)} %bitcast.26, bf16[924,8192]{1,0:T(8,128)(2,1)} %reshape.184), kind=kOutput, calls=%fused_computation.2 | convolution fusion | flops 15510536192 | bytes 33808384 | tf_op jit(solution)/shard_map/dot_general | solution.py:86
  83.4 4.3 %all-to-all-start.1 = ((s32[4,1,24]{2,1,0:T(1,128)}), s32[4,1,24]{2,1,0:T(1,128)S(1)}, u32[]{:S(2)}, u32[]{:S(2)}) async-start(s32[4,1,24]{2,1,0:T(1,128)} %bitcast.4), calls=%async_computation.2 | async-start | bytes 4096 | tf_op jit(solution)/shard_map/all_to_all | solution.py:105
  87.8 2.6 convolution_convert_fusion.1
  90.3 2.6 all-to-all-done.1
  92.9 3.7 %all-to-all-start.3 = ((bf16[4,24,14784]{2,1,0:T(8,128)(2,1)}), bf16[4,24,14784]{2,1,0:T(8,128)(2,1)S(1)}, u32[]{:S(2)}, u32[]{:S(2)}) async-start(bf16[4,24,14784]{2,1,0:T(8,128)(2,1)} %bitcast.22), calls=%async_computation.4 | async-start | bytes 5701632 | tf_op jit(solution)/shard_map/all_to_all | solution.py:102
  99.3 31.0 %all-to-all-done.3 = bf16[4,24,14784]{2,1,0:T(8,128)(2,1)S(1)} async-done(((bf16[4,24,14784]{2,1,0:T(8,128)(2,1)}), bf16[4,24,14784]{2,1,0:T(8,128)(2,1)S(1)}, u32[]{:S(2)}, u32[]{:S(2)}) %all-to-all-start.3) | async-done | bytes 2838560 | tf_op jit(solution)/shard_map/all_to_all | solution.py:102
  130.3 7.3 %all-to-all-start.2 = ((s32[32,1,3]{2,1,0:T(1,128)}), s32[32,1,3]{2,1,0:T(1,128)S(1)}, u32[]{:S(2)}, u32[]{:S(2)}) async-start(s32[32,1,3]{2,1,0:T(1,128)} %bitcast.5), calls=%async_computation.3 | async-start | bytes 32768 | tf_op jit(solution)/shard_map/all_to_all | solution.py:133
  137.6 2.8 convolution_convert_fusion
  140.4 3.1 %reshape.178 = bf16[32,3,14784]{2,1,0:T(4,128)(2,1)} reshape(bf16[96,14784]{1,0:T(8,128)(2,1)S(1)} %convolution_convert_fusion) | data formatting | bytes 5677056 | tf_op jit(solution)/shard_map/reshape | solution.py:127
  143.5 1.6 all-to-all-done.2
  145.1 6.0 %all-to-all-start.4 = ((bf16[32,3,14784]{2,1,0:T(4,128)(2,1)}), bf16[32,3,14784]{2,1,0:T(4,128)(2,1)}, u32[]{:S(2)}, u32[]{:S(2)}) async-start(bf16[32,3,14784]{2,1,0:T(4,128)(2,1)} %reshape.178), calls=%async_computation.5 | async-start | bytes 7602176 | tf_op jit(solution)/shard_map/all_to_all | solution.py:126
  152.4 55.6 %all-to-all-done.4 = bf16[32,3,14784]{2,1,0:T(4,128)(2,1)} async-done(((bf16[32,3,14784]{2,1,0:T(4,128)(2,1)}), bf16[32,3,14784]{2,1,0:T(4,128)(2,1)}, u32[]{:S(2)}, u32[]{:S(2)}) %all-to-all-start.4) | async-done | bytes 2838560 | tf_op jit(solution)/shard_map/all_to_all | solution.py:126
  208.0 4.3 %reshape.179 = bf16[96,14784]{1,0:T(8,128)(2,1)S(1)} reshape(bf16[32,3,14784]{2,1,0:T(4,128)(2,1)} %all-to-all-done.4) | data formatting | bytes 5677056 | tf_op jit(solution)/shard_map/reshape | solution.py:141
  212.3 12.8 %convolution_convert_fusion.4 = bf16[96,8192]{1,0:T(8,128)(2,1)} fusion(bf16[320,8192]{1,0:T(8,128)(2,1)} %param.13, bf16[96,14784]{1,0:T(8,128)(2,1)S(1)} %reshape.179, bf16[14784,320]{0,1:T(8,128)(2,1)} %param.12, f32[96]{0:T(128)S(1)} %select_reduce_fusion.1, s32[96]{0:T(128)S(1)} %add.93, s32[96]{0:T(128)S(1)} %get-tuple-element.6), kind=kOutput, calls=%fused_computation.4 | convolution fusion | flops 1412616192 | bytes 19117184 | tf_op jit(solution)/shard_map/dot_general | solution.py:54
  225.1 2.7 convert_element_type.49
  227.8 32.3 %all_to_all.47 = bf16[32,3,8192]{2,1,0:T(4,128)(2,1)} all-to-all(bf16[32,3,8192]{2,1,0:T(4,128)(2,1)S(1)} %convert_element_type.49), channel_id=1, replica_groups=mesh['dp'=4,'tp'=32] {'tp'}, dimensions={0} | all-to-all | bytes 3145728 | tf_op jit(solution)/shard_map/all_to_all | solution.py:149
  260.1 3.2 %reshape.180 = bf16[96,8192]{1,0:T(8,128)(2,1)S(1)} reshape(bf16[32,3,8192]{2,1,0:T(4,128)(2,1)} %all_to_all.47) | data formatting | bytes 3145728 | tf_op jit(solution)/shard_map/reshape | solution.py:158
  263.9 25.1 %all_to_all.48 = bf16[4,24,8192]{2,1,0:T(8,128)(2,1)S(1)} all-to-all(bf16[4,24,8192]{2,1,0:T(8,128)(2,1)S(1)} %bitcast.25), channel_id=1, replica_groups=mesh['dp'=4,'tp'=32] {'dp'}, dimensions={0} | all-to-all | bytes 3145728 | tf_op jit(solution)/shard_map/all_to_all | solution.py:161
  289.0 2.7 fusion
  (47 shorter events, 7.3 us)
Async XLA Ops:
  6.5 35.4 %all-gather.3.cloned.1.call-start = ((), (), s32[]{:S(2)}) async-start(), calls=%async_computation.9 | async-start | bytes 22806528 | tf_op jit(solution)/shard_map/all_gather | solution.py:76
  15.1 41.0 %all-to-all-start = ((bf16[64,16,924]{2,0,1:T(8,128)(2,1)}), bf16[64,16,924]{2,0,1:T(8,128)(2,1)S(1)}, u32[]{:S(2)}, u32[]{:S(2)}) async-start(bf16[64,16,924]{2,0,1:T(8,128)(2,1)} %copy.12), calls=%async_computation | async-start | bytes 4194304 | tf_op jit(solution)/shard_map/all_to_all | solution.py:77
  23.2 265.8 %reduce-scatter.2.cloned.1.call-start = ((), (), s32[]{:S(2)}) async-start(), calls=%async_computation.8 | async-start | bytes 17825792 | tf_op jit(solution)/shard_map/reduce_scatter | solution.py:85
  81.4 0.7 copy-start.2
  81.4 0.7 copy-start.4
  81.4 6.4 %copy-start.1 = (bf16[64,14784]{1,0:T(8,128)(2,1)S(1)}, bf16[64,14784]{1,0:T(8,128)(2,1)}, u32[]{:S(2)}) copy-start(bf16[64,14784]{1,0:T(8,128)(2,1)} %param.7) | copy-start | bytes 5677060
  83.4 9.5 %all-to-all-start.1 = ((s32[4,1,24]{2,1,0:T(1,128)}), s32[4,1,24]{2,1,0:T(1,128)S(1)}, u32[]{:S(2)}, u32[]{:S(2)}) async-start(s32[4,1,24]{2,1,0:T(1,128)} %bitcast.4), calls=%async_computation.2 | async-start | bytes 4096 | tf_op jit(solution)/shard_map/all_to_all | solution.py:105
  92.9 37.4 %all-to-all-start.3 = ((bf16[4,24,14784]{2,1,0:T(8,128)(2,1)}), bf16[4,24,14784]{2,1,0:T(8,128)(2,1)S(1)}, u32[]{:S(2)}, u32[]{:S(2)}) async-start(bf16[4,24,14784]{2,1,0:T(8,128)(2,1)} %bitcast.22), calls=%async_computation.4 | async-start | bytes 5701632 | tf_op jit(solution)/shard_map/all_to_all | solution.py:102
  130.3 7.3 %copy-start = (bf16[4,24,14784]{2,1,0:T(8,128)(2,1)}, bf16[4,24,14784]{2,1,0:T(8,128)(2,1)S(1)}, u32[]{:S(2)}) copy-start(bf16[4,24,14784]{2,1,0:T(8,128)(2,1)S(1)} %all-to-all-done.3) | copy-start | bytes 8515588
  130.3 14.8 %all-to-all-start.2 = ((s32[32,1,3]{2,1,0:T(1,128)}), s32[32,1,3]{2,1,0:T(1,128)S(1)}, u32[]{:S(2)}, u32[]{:S(2)}) async-start(s32[32,1,3]{2,1,0:T(1,128)} %bitcast.5), calls=%async_computation.3 | async-start | bytes 32768 | tf_op jit(solution)/shard_map/all_to_all | solution.py:133
  143.5 7.6 %copy-start.3 = (s32[256]{0:T(256)S(1)}, s32[256]{0:T(256)}, u32[]{:S(2)}) copy-start(s32[256]{0:T(256)} %param.9) | copy-start | bytes 3076
  145.1 62.9 %all-to-all-start.4 = ((bf16[32,3,14784]{2,1,0:T(4,128)(2,1)}), bf16[32,3,14784]{2,1,0:T(4,128)(2,1)}, u32[]{:S(2)}, u32[]{:S(2)}) async-start(bf16[32,3,14784]{2,1,0:T(4,128)(2,1)} %reshape.178), calls=%async_computation.5 | async-start | bytes 7602176 | tf_op jit(solution)/shard_map/all_to_all | solution.py:126
Sparse Core Ops, SparseCore 0:
  9.0 32.8 all-gather.2
  81.5 152.9 reduce-scatter.1

commit v2 on v0

v2 whole, which is shorter than its diff:
```python
import functools

import jax
import jax.numpy as jnp
from jax import lax
from jax.experimental import pallas as pl
from jax.experimental.pallas import tpu as pltpu
from jax.sharding import PartitionSpec as P

MESH = pl.DeviceIdType.MESH
BF16 = jnp.bfloat16
F32 = jnp.float32
adapter_scale_fn = 4.0

RING = 4
CHIPS = RING * RING
TP = 2 * CHIPS
HOME = 64
CAP = 24
OWN = 3
SLOTS = RING * CAP
LANES = 512
TILE = 512
SLAB_ROWS = TP
OUT_ROWS = 16


def prefix_count(match):
    n = match.shape[0]
    order = jnp.arange(n, dtype=jnp.int32)
    tri = (order[None, :] <= order[:, None]).astype(BF16)
    return jnp.dot(tri, match.astype(BF16), preferred_element_type=F32).astype(jnp.int32)


def lookup(index, table):
    hit = index[:, None] == jnp.arange(table.shape[0], dtype=jnp.int32)[None, :]
    return jnp.sum(jnp.where(hit, table[None, :], 0), axis=1)


def place(target, value, size):
    hit = jnp.arange(size, dtype=jnp.int32)[:, None] == target[None, :]
    return jnp.sum(jnp.where(hit, value[None, :], 0), axis=1)


def routing(draft_row_client, client_rank_bin, client_device):
    x, t = lax.axis_index("dp"), lax.axis_index("tp")
    slots = jnp.arange(SLOTS, dtype=jnp.int32)

    def send(values, axis, parts):
        return lax.all_to_all(
            values.reshape(parts, SLOTS // parts), axis, split_axis=0, concat_axis=0, tiled=True
        ).reshape(SLOTS)

    group = lookup(draft_row_client, client_device) // TP
    hit = group[:, None] == jnp.arange(RING, dtype=jnp.int32)[None, :]
    rank = jnp.sum(jnp.where(hit, prefix_count(hit) - 1, 0), axis=1)
    slot_of_row = group * CAP + rank
    home_index = place(slot_of_row, jnp.arange(HOME, dtype=jnp.int32), SLOTS)

    tenant = send(place(slot_of_row, draft_row_client + 1, SLOTS), "dp", RING) - 1
    position = lookup(tenant, client_device) % TP
    hit = (position[:, None] == jnp.arange(TP, dtype=jnp.int32)[None, :]) & (tenant >= 0)[:, None]
    rank = jnp.sum(jnp.where(hit, prefix_count(hit) - 1, 0), axis=1)
    owner = jnp.where(tenant >= 0, position * OWN + rank, -1)
    owner_index = place(owner, slots, SLOTS)
    back_index = jnp.maximum(owner, 0)

    tenant = send(place(owner, tenant + 1, SLOTS), "tp", TP) - 1
    tenant_id = jnp.arange(client_device.shape[0], dtype=jnp.int32)
    first = jnp.min(jnp.where(client_device == x * TP + t, tenant_id, client_device.shape[0]))
    first_rank = jnp.sum(jnp.where(tenant_id == first, client_rank_bin, 0))
    start = jnp.where(tenant == first, 0, first_rank)
    count = lookup(tenant, client_rank_bin)
    gain = jnp.where(
        count > 0, adapter_scale_fn / jnp.sqrt(jnp.maximum(count, 1).astype(F32)), 0.0
    )
    return home_index, owner_index, back_index, slot_of_row, start, count, gain


def body(
    index,
    gains,
    rows_in,
    slabs_in,
    weight_in,
    down_in,
    down_tail,
    up_in,
    out,
    fin_hbm,
    xrecv,
    weight,
    packed,
    gathered,
    owned,
    wide,
    down,
    up,
    back_out,
    back_in,
    home_out,
    home_in,
    parts,
    relay,
    second_out,
    second_in,
    own_sum,
    local_sem,
    down_sem,
    up_sem,
    w_sem,
    x_send,
    x_recv,
    a_send,
    a_recv,
    t_send,
    t_recv,
    b_send,
    b_recv,
    c_send,
    c_recv,
    r_send,
    r_recv,
    s_send,
    s_recv,
):
    width = weight.shape[2]
    depth = weight.shape[1]
    half = width // 4
    x, t = lax.axis_index("dp"), lax.axis_index("tp")
    z, y, core, chip = t // 8, (t // 2) % 4, t % 2, t // 2

    quarters = wide.shape[0]

    def put_wide(at, value):
        for j in range(quarters):
            wide[j, at, :] = value[:, j * 128 : (j + 1) * 128]

    def get_wide(at):
        return jnp.concatenate([wide[j, at, :] for j in range(quarters)], axis=1)

    def remote(src, dst, send, recv, device):
        return pltpu.make_async_remote_copy(
            src_ref=src,
            dst_ref=dst,
            send_sem=send,
            recv_sem=recv,
            device_id=device,
            device_id_type=MESH,
        )

    barrier = pltpu.get_barrier_semaphore()

    @pl.loop(1, TP)
    def _(i):
        pl.semaphore_signal(barrier, inc=1, device_id=(x, (t + i) % TP), device_id_type=MESH)

    @pl.loop(1, RING)
    def _(i):
        pl.semaphore_signal(barrier, inc=1, device_id=((x + i) % RING, t), device_id_type=MESH)

    pl.semaphore_wait(barrier, TP - 1 + RING - 1)

    def x_copy(peer, slot):
        return remote(
            slabs_in.at[peer], xrecv.at[slot], x_send.at[peer], x_recv.at[slot], (x, 2 * peer + core)
        )

    @pl.loop(1, CHIPS)
    def _(i):
        peer = (chip + i) % CHIPS
        x_copy(peer, chip).start()

    x_own = pltpu.make_async_copy(slabs_in.at[chip], xrecv.at[chip], local_sem.at[0])
    x_own.start()
    w_out = remote(weight_in, weight.at[core], w_sem.at[0], w_sem.at[1], (x, t + 1 - 2 * core))
    w_out.start()
    w_own = pltpu.make_async_copy(weight_in, weight.at[core], local_sem.at[1])
    w_own.start()

    @pl.loop(0, SLOTS)
    def _(i):
        packed[i] = rows_in[index[0, i]]

    def a_copy(peer, slot):
        return remote(
            packed.at[pl.ds(peer * CAP, CAP)],
            gathered.at[pl.ds(slot * CAP, CAP)],
            a_send.at[peer],
            a_recv.at[slot],
            (peer, t),
        )

    @pl.loop(1, RING)
    def _(i):
        a_copy((x + i) % RING, x).start()

    a_own = pltpu.make_async_copy(
        packed.at[pl.ds(x * CAP, CAP)], gathered.at[pl.ds(x * CAP, CAP)], local_sem.at[2]
    )
    a_own.start()
    a_own.wait()

    @pl.loop(1, RING)
    def _(i):
        peer = (x + i) % RING
        a_copy(peer, peer).wait_recv()

    @pl.loop(1, RING)
    def _(i):
        peer = (x + i) % RING
        a_copy(peer, peer).wait_send()

    @pl.loop(0, SLOTS)
    def _(i):
        packed[i] = gathered[index[1, i]]

    def t_copy(peer, slot):
        return remote(
            packed.at[pl.ds(peer * OWN, OWN)],
            owned.at[pl.ds(slot * OWN, OWN)],
            t_send.at[peer],
            t_recv.at[slot],
            (x, peer),
        )

    @pl.loop(1, TP)
    def _(i):
        t_copy((t + i) % TP, t).start()

    t_own = pltpu.make_async_copy(
        packed.at[pl.ds(t * OWN, OWN)], owned.at[pl.ds(t * OWN, OWN)], local_sem.at[2]
    )
    t_own.start()

    w_own.wait()
    w_out.wait()
    x_own.wait()

    @pl.loop(1, CHIPS)
    def _(i):
        peer = (chip + i) % CHIPS
        x_copy(peer, peer).wait_recv()

    def axes(p):
        return (y, z) if p == 0 else (z, y)

    def device(p, a, b):
        return (x, (b * RING + a if p == 0 else a * RING + b) * 2 + core)

    def partial_sum(p, a_to, column):
        b = axes(p)[1]
        total = None
        for k in range(2):
            left = []
            for i in range(RING):
                b_to = (b + i) % RING
                at = b_to * RING + a_to if p == 0 else a_to * RING + b_to
                left.append(xrecv[at, k * HOME : (k + 1) * HOME, :][:, :depth])
            term = jnp.dot(
                jnp.concatenate(left, axis=0),
                weight[k, :, pl.ds(column, TILE)],
                preferred_element_type=F32,
            )
            total = term if total is None else total + term
        return total

    def fill(p, slot, a_to, side, added=None):
        @pl.loop(0, half // TILE)
        def _(n):
            col = pl.multiple_of(n * TILE, TILE)
            total = partial_sum(p, a_to, pl.multiple_of((2 * p + side) * half + n * TILE, TILE))
            if added is not None:
                total = total + relay[p, added, :, pl.ds(col, TILE)].astype(F32)
            parts[p, slot, :, pl.ds(col, TILE)] = total.astype(BF16)

    def r_copy(p, k):
        a, b = axes(p)
        up_to, down_to = device(p, (a + 1) % RING, b), device(p, (a + 3) % RING, b)
        src, dst, to = [
            (0, relay.at[p, 0], up_to),
            (1, relay.at[p, 1], down_to),
            (2, fin_hbm.at[p, 1], up_to),
            (3, fin_hbm.at[p, 2], down_to),
            (0, fin_hbm.at[p, 0], up_to),
            (1, fin_hbm.at[p, 3], down_to),
        ][k]
        return remote(parts.at[p, src], dst, r_send.at[p, k], r_recv.at[p, k], to)

    for p in range(2):
        a, b = axes(p)
        for k in range(2):
            fill(p, k, (a + 2) % RING, k)
            r_copy(p, k).start()
    for p in range(2):
        a, b = axes(p)
        fill(p, 2, (a + 1) % RING, 1)
        r_copy(p, 2).start()
        fill(p, 3, (a + 3) % RING, 0)
        r_copy(p, 3).start()
    for p in range(2):
        a, b = axes(p)
        for k in range(2):
            r_copy(p, k).wait()
            fill(p, k, (a + 1 + 2 * k) % RING, k, added=k)
            r_copy(p, 4 + k).start()

    t_own.wait()

    @pl.loop(1, TP)
    def _(i):
        peer = (t + i) % TP
        t_copy(peer, peer).wait_recv()

    chunks = down_in.shape[1] // LANES

    def down_copy(s):
        return pltpu.make_async_copy(
            down_in.at[:, pl.ds(pl.multiple_of(s * LANES, LANES), LANES)],
            down.at[s % 2],
            down_sem.at[s % 2],
        )

    def up_copy(s):
        return pltpu.make_async_copy(
            up_in.at[:, pl.ds(pl.multiple_of(s * TILE, TILE), TILE)], up.at[s % 2], up_sem.at[s % 2]
        )

    down_copy(0).start()
    up_copy(0).start()
    part = SLOTS // 2
    for k in range(2):

        @pl.loop(0, part)
        def _(i):
            put_wide(pl.ds(i * SLAB_ROWS, SLAB_ROWS), owned[k * part + i].astype(F32))

        @pl.loop(0, chunks + 1)
        def _(s):
            piece = get_wide(pl.ds(s, part, stride=SLAB_ROWS)).astype(BF16)
            for j in range(OWN):
                lo, hi = max(j * SLAB_ROWS, k * part), min((j + 1) * SLAB_ROWS, (k + 1) * part)
                if lo < hi:
                    gathered[s * OWN + j, lo - j * SLAB_ROWS : hi - j * SLAB_ROWS, :] = piece[
                        lo - k * part : hi - k * part
                    ]

    def latent_term(s, factors):
        left = gathered[pl.ds(s * OWN, OWN)].reshape(SLOTS, LANES)
        return lax.dot_general(left, factors, (((1,), (1,)), ((), ())), preferred_element_type=F32)

    def latent_step(s, total):
        @pl.when(s + 1 < chunks)
        def _():
            down_copy(s + 1).start()

        down_copy(s).wait()
        return total + latent_term(s, down[s % 2])

    latent = lax.fori_loop(0, chunks, latent_step, latent_term(chunks, down_tail[...]))
    latent = (latent * gains[...]).astype(BF16)

    @pl.loop(0, OUT_ROWS)
    def _(s):
        @pl.when(s + 1 < OUT_ROWS)
        def _():
            up_copy(s + 1).start()

        up_copy(s).wait()
        put_wide(
            pl.ds(s, SLOTS, stride=OUT_ROWS),
            jnp.dot(latent, up[s % 2], preferred_element_type=F32),
        )

    @pl.loop(0, SLOTS)
    def _(i):
        back_out[i] = get_wide(pl.ds(i * OUT_ROWS, OUT_ROWS)).astype(BF16)

    def b_copy(peer, slot):
        return remote(
            back_out.at[pl.ds(peer * OWN, OWN)],
            back_in.at[pl.ds(slot * OWN, OWN)],
            b_send.at[peer],
            b_recv.at[slot],
            (x, peer),
        )

    @pl.loop(1, TP)
    def _(i):
        b_copy((t + i) % TP, t).start()

    b_own = pltpu.make_async_copy(
        back_out.at[pl.ds(t * OWN, OWN)], back_in.at[pl.ds(t * OWN, OWN)], local_sem.at[2]
    )
    b_own.start()

    def s_copy(p, d):
        a, b = axes(p)
        return remote(
            second_out.at[p, d - 1],
            second_in.at[p, d - 1],
            s_send.at[p, d - 1],
            s_recv.at[p, d - 1],
            device(p, a, (b + d) % RING),
        )

    for p in range(2):
        a, b = axes(p)
        for k in range(2):
            r_copy(p, 2 + k).wait()
            r_copy(p, 4 + k).wait()
        fin = pltpu.make_async_copy(fin_hbm.at[p], parts.at[p], local_sem.at[3])
        fin.start()
        fin.wait()
        for side in range(2):

            @pl.loop(0, half // TILE)
            def _(n):
                col = pl.multiple_of(n * TILE, TILE)
                at = pl.multiple_of(side * half + n * TILE, TILE)
                total = partial_sum(p, a, pl.multiple_of((2 * p + side) * half + n * TILE, TILE))
                total = total + parts[p, side, :, pl.ds(col, TILE)].astype(F32)
                total = total + parts[p, 2 + side, :, pl.ds(col, TILE)].astype(F32)
                own_sum[p, :, pl.ds(at, TILE)] = total[:HOME]
                for d in range(1, RING):
                    second_out[p, d - 1, :, pl.ds(at, TILE)] = total[
                        d * HOME : (d + 1) * HOME
                    ].astype(BF16)

        for d in range(1, RING):
            s_copy(p, d).start()

    b_own.wait()

    @pl.loop(1, TP)
    def _(i):
        peer = (t + i) % TP
        b_copy(peer, peer).wait_recv()

    @pl.loop(0, SLOTS)
    def _(i):
        home_out[i] = back_in[index[2, i]]

    def c_copy(peer, slot):
        return remote(
            home_out.at[pl.ds(peer * CAP, CAP)],
            home_in.at[pl.ds(slot * CAP, CAP)],
            c_send.at[peer],
            c_recv.at[slot],
            (peer, t),
        )

    @pl.loop(1, RING)
    def _(i):
        c_copy((x + i) % RING, x).start()

    c_own = pltpu.make_async_copy(
        home_out.at[pl.ds(x * CAP, CAP)], home_in.at[pl.ds(x * CAP, CAP)], local_sem.at[2]
    )
    c_own.start()

    for p in range(2):
        for d in range(1, RING):
            s_copy(p, d).wait()
    c_own.wait()

    @pl.loop(1, RING)
    def _(i):
        peer = (x + i) % RING
        c_copy(peer, peer).wait_recv()

    @pl.loop(0, HOME)
    def _(i):
        put_wide(pl.ds(i * OUT_ROWS, OUT_ROWS), home_in[index[3, i]].astype(F32))

    for p in range(2):

        @pl.loop(0, OUT_ROWS // 2)
        def _(n):
            at = pl.multiple_of(n * TILE, TILE)
            total = own_sum[p, :, pl.ds(at, TILE)]
            for d in range(3):
                total = total + second_in[p, d, :, pl.ds(at, TILE)].astype(F32)
            total = total + get_wide(pl.ds(p * (OUT_ROWS // 2) + n, HOME, stride=OUT_ROWS))
            out[:, pl.ds(pl.multiple_of(p * 2 * half + n * TILE, TILE), TILE)] = total.astype(BF16)

    @pl.loop(1, CHIPS)
    def _(i):
        peer = (chip + i) % CHIPS
        x_copy(peer, peer).wait_send()

    @pl.loop(1, TP)
    def _(i):
        peer = (t + i) % TP
        t_copy(peer, peer).wait_send()
        b_copy(peer, peer).wait_send()

    @pl.loop(1, RING)
    def _(i):
        peer = (x + i) % RING
        c_copy(peer, peer).wait_send()


def local(
    hidden,
    draft_row_client,
    client_rank_bin,
    client_device,
    down_weight,
    packed_down_factors,
    packed_up_factors,
):
    depth, width = down_weight.shape
    rank_columns = packed_down_factors.shape[1]
    home_index, owner_index, back_index, final_index, start, count, gain = routing(
        draft_row_client, client_rank_bin, client_device
    )
    index = jnp.stack(
        [home_index, owner_index, back_index, jnp.pad(final_index, (0, SLOTS - HOME))]
    ).astype(jnp.int32)
    span = jnp.arange(rank_columns, dtype=jnp.int32)[None, :]
    inside = (span >= start[:, None]) & (span < (start + count)[:, None])
    gains = jnp.where(inside, gain[:, None], 0.0)
    units = hidden.shape[1]
    rows = jnp.pad(hidden, ((0, 0), (0, SLAB_ROWS * LANES - units)))
    rows = rows.reshape(HOME, SLAB_ROWS, LANES)
    slabs = jnp.pad(hidden.reshape(HOME, TP, depth), ((0, 0), (0, 0), (0, LANES - depth)))
    slabs = jnp.transpose(slabs, (1, 0, 2)).reshape(CHIPS, 2 * HOME, LANES)
    down = packed_down_factors.T
    tail = units // LANES * LANES
    down_tail = jnp.pad(down[:, tail:], ((0, 0), (0, LANES - units + tail)))

    vmem, hbm = pl.BlockSpec(memory_space=pltpu.VMEM), pl.BlockSpec(memory_space=pl.ANY)
    dma = pltpu.SemaphoreType.DMA
    half = width // 4
    out, _ = pl.pallas_call(
        body,
        out_shape=(
            jax.ShapeDtypeStruct((HOME, width), BF16),
            jax.ShapeDtypeStruct((2, 4, RING * HOME, half), BF16),
        ),
        in_specs=[pl.BlockSpec(memory_space=pltpu.SMEM), vmem, vmem, hbm, hbm, hbm, vmem, hbm],
        out_specs=(vmem, hbm),
        scratch_shapes=[
            pltpu.VMEM((CHIPS, 2 * HOME, LANES), BF16),
            pltpu.VMEM((2, depth, width), BF16),
            pltpu.VMEM((SLOTS, SLAB_ROWS, LANES), BF16),
            pltpu.VMEM((SLOTS, SLAB_ROWS, LANES), BF16),
            pltpu.VMEM((SLOTS, SLAB_ROWS, LANES), BF16),
            pltpu.VMEM((TILE // 128, SLOTS * OUT_ROWS, 128), F32),
            pltpu.VMEM((2, rank_columns, LANES), BF16),
            pltpu.VMEM((2, rank_columns, TILE), BF16),
            pltpu.VMEM((SLOTS, OUT_ROWS, TILE), BF16),
            pltpu.VMEM((SLOTS, OUT_ROWS, TILE), BF16),
            pltpu.VMEM((SLOTS, OUT_ROWS, TILE), BF16),
            pltpu.VMEM((SLOTS, OUT_ROWS, TILE), BF16),
            pltpu.VMEM((2, 4, RING * HOME, half), BF16),
            pltpu.VMEM((2, 2, RING * HOME, half), BF16),
            pltpu.VMEM((2, 3, HOME, 2 * half), BF16),
            pltpu.VMEM((2, 3, HOME, 2 * half), BF16),
            pltpu.VMEM((2, HOME, 2 * half), F32),
            dma((4,)),
            dma((2,)),
            dma((2,)),
            dma((2,)),
            dma((CHIPS,)),
            dma((CHIPS,)),
            dma((RING,)),
            dma((RING,)),
            dma((TP,)),
            dma((TP,)),
            dma((TP,)),
            dma((TP,)),
            dma((RING,)),
            dma((RING,)),
            dma((2, 6)),
            dma((2, 6)),
            dma((2, 3)),
            dma((2, 3)),
        ],
        compiler_params=pltpu.CompilerParams(
            collective_id=0, has_side_effects=True, vmem_limit_bytes=63 << 20
        ),
        name="verify_rows",
    )(index, gains, rows, slabs, down_weight, down, down_tail, packed_up_factors)
    return out


def solution(mesh):
    placed = (
        P(("dp", "tp"), None),
        P(("dp", "tp")),
        P(),
        P(),
        P("tp", None),
        P(None, ("dp", "tp")),
        P(("dp", "tp"), None),
    )
    return jax.shard_map(
        local, mesh=mesh, in_specs=placed, out_specs=P(("dp", "tp"), None), check_vma=False
    )
```

time: 586 us -> 261 us (0.45)
  the two profiles are of different devices: /device:TPU:0 before, /device:TPU:25 now
where the time goes in v2:
time: 261 us; the launch traced here: 260 us
  Pallas kernels  215 us (82%)
  local copies, waits for them, and re-layouts  18.5 us (7%)
  starting transfers between devices  12.9 us (5%)
  other arithmetic  8.19 us (3%)
  waiting for transfers between devices  4.69 us (2%)
    pallas_call x1, Pallas kernels, local(): pl.pallas_call(body, out_shape=(jax.ShapeDtypeStruct((HOME, width), BF16)...  215 us
    all_to_all x2, starting transfers between devices, send(): lax.all_to_all(values.reshape(parts, SLOTS // parts), axis, split_axis=0,...  12.9 us
    reshape x2, local copies, waits for them, and re-layouts, local(): hidden.reshape(HOME, TP, depth)  6.72 us
  transfers between devices with their start and end apart: 2, of which 1 were waited for; matrix products, arithmetic and copies ran while one was open for 7% of the time, Pallas kernels for 0%

profile of v2, /device:TPU:25, one launch (start us, length us, event | category | flops | bytes accessed | tf_op | source)
XLA Modules:
  0.0 259.6 jit_solution(7796249621152541266)
XLA Ops:
  0.0 0.9 select_reduce_fusion.2
  1.0 0.7 multiply_add_fusion
  1.8 0.7 all_to_all.12
  2.5 4.0 %all-to-all-start = ((s32[4,1,24]{2,1,0:T(1,128)}), s32[4,1,24]{2,1,0:T(1,128)S(1)}, u32[]{:S(2)}, u32[]{:S(2)}) async-start(s32[4,1,24]{2,1,0:T(1,128)} %bitcast.1), calls=%async_computation | async-start | bytes 4096 | tf_op jit(solution)/shard_map/all_to_all | solution.py:50
  6.5 1.3 fusion.12
  7.9 1.0 slice.4
  8.8 5.6 %reshape.203 = bf16[64,32,462]{2,1,0:T(8,128)(2,1)S(1)} reshape(bf16[64,14784]{1,0:T(8,128)(2,1)} %param.7) | data formatting | bytes 3784704 | tf_op jit(solution)/shard_map/reshape | solution.py:527
  14.4 1.7 pad.17
  16.1 1.3 fusion.13
  17.4 0.8 pad.19.down_tail
  18.2 1.2 copy.18
  19.3 1.7 pad.18
  21.0 2.2 copy.19
  23.2 0.6 broadcast.332
  23.8 0.7 reduce.9
  25.2 0.7 all_to_all.14
  25.9 8.9 %all-to-all-start.1 = ((s32[32,1,3]{2,1,0:T(1,128)}), s32[32,1,3]{2,1,0:T(1,128)S(1)}, u32[]{:S(2)}, u32[]{:S(2)}) async-start(s32[32,1,3]{2,1,0:T(1,128)} %bitcast.6), calls=%async_computation.1 | async-start | bytes 32768 | tf_op jit(solution)/shard_map/all_to_all | solution.py:50
  34.8 0.6 pad_add_fusion.index
  35.4 4.7 %all-to-all-done.1 = s32[32,1,3]{2,1,0:T(1,128)S(1)} async-done(((s32[32,1,3]{2,1,0:T(1,128)}), s32[32,1,3]{2,1,0:T(1,128)S(1)}, u32[]{:S(2)}, u32[]{:S(2)}) %all-to-all-start.1) | async-done | bytes 416 | tf_op jit(solution)/shard_map/all_to_all | solution.py:50
  40.2 0.2 select_reduce_fusion
  40.4 1.3 fusion.21
  41.7 0.8 fusion.7.gains
  42.5 214.8 %verify_rows.1 = (bf16[64,8192]{1,0:T(8,128)(2,1)}, bf16[2,4,256,2048]{3,2,1,0:T(8,128)(2,1)}) custom-call(s32[4,96]{1,0:T(4,128)} %pad_add_fusion.index, f32[96,320]{1,0:T(8,128)} %fusion.7.gains, bf16[64,32,512]{2,1,0:T(8,128)(2,1)} %bitcast.23, bf16[16,128,512]{2,1,0:T(8,128)(2,1)} %bitcast.22, bf16[462,8192]{1,0:T(8,128)(2,1)} %weight_in.1, ...), custom_call_target="tpu_custom_call" | custom-call | tf_op jit(solution)/shard_map/verify_rows/pallas_call | solution.py:536
  257.3 2.3 copy.21
  (23 shorter events, 1.1 us)
Async XLA Ops:
  2.5 20.7 %all-to-all-start = ((s32[4,1,24]{2,1,0:T(1,128)}), s32[4,1,24]{2,1,0:T(1,128)S(1)}, u32[]{:S(2)}, u32[]{:S(2)}) async-start(s32[4,1,24]{2,1,0:T(1,128)} %bitcast.1), calls=%async_computation | async-start | bytes 4096 | tf_op jit(solution)/shard_map/all_to_all | solution.py:50
  14.4 1.7 copy-start.1
  21.0 3.7 %copy-start = (s32[256]{0:T(256)S(1)}, s32[256]{0:T(256)}, u32[]{:S(2)}) copy-start(s32[256]{0:T(256)} %param.10) | copy-start | bytes 3076
  25.9 14.2 %all-to-all-start.1 = ((s32[32,1,3]{2,1,0:T(1,128)}), s32[32,1,3]{2,1,0:T(1,128)S(1)}, u32[]{:S(2)}, u32[]{:S(2)}) async-start(s32[32,1,3]{2,1,0:T(1,128)} %bitcast.6), calls=%async_computation.1 | async-start | bytes 32768 | tf_op jit(solution)/shard_map/all_to_all | solution.py:50

commit v3 on v2

v3 whole, which is shorter than its diff:
```python
import functools

import jax
import jax.numpy as jnp
from jax import lax
from jax.experimental import pallas as pl
from jax.experimental.pallas import tpu as pltpu
from jax.sharding import PartitionSpec as P

MESH = pl.DeviceIdType.MESH
BF16 = jnp.bfloat16
F32 = jnp.float32
adapter_scale_fn = 4.0

RING = 4
CHIPS = RING * RING
TP = 2 * CHIPS
HOME = 64
CAP = 24
OWN = 3
SLOTS = RING * CAP
LANES = 512
TILE = 512
SLAB_ROWS = TP
PART = SLAB_ROWS // 2
OUT = 256
AHEAD = 8
UP_AHEAD = 4


def prefix_count(match):
    n = match.shape[0]
    order = jnp.arange(n, dtype=jnp.int32)
    tri = (order[None, :] <= order[:, None]).astype(BF16)
    return jnp.dot(tri, match.astype(BF16), preferred_element_type=F32).astype(jnp.int32)


def lookup(index, table):
    hit = index[:, None] == jnp.arange(table.shape[0], dtype=jnp.int32)[None, :]
    return jnp.sum(jnp.where(hit, table[None, :], 0), axis=1)


def place(target, value, size):
    hit = jnp.arange(size, dtype=jnp.int32)[:, None] == target[None, :]
    return jnp.sum(jnp.where(hit, value[None, :], 0), axis=1)


def routing(draft_row_client, client_rank_bin, client_device, rank_columns):
    x, t = lax.axis_index("dp"), lax.axis_index("tp")
    slots = jnp.arange(SLOTS, dtype=jnp.int32)

    def send(values, axis, parts):
        return lax.all_to_all(
            values.reshape(parts, SLOTS // parts), axis, split_axis=0, concat_axis=0, tiled=True
        ).reshape(SLOTS)

    group = lookup(draft_row_client, client_device) // TP
    hit = group[:, None] == jnp.arange(RING, dtype=jnp.int32)[None, :]
    rank = jnp.sum(jnp.where(hit, prefix_count(hit) - 1, 0), axis=1)
    slot_of_row = group * CAP + rank
    home_index = place(slot_of_row, jnp.arange(HOME, dtype=jnp.int32), SLOTS)

    tenant = send(place(slot_of_row, draft_row_client + 1, SLOTS), "dp", RING) - 1
    position = lookup(tenant, client_device) % TP
    hit = (position[:, None] == jnp.arange(TP, dtype=jnp.int32)[None, :]) & (tenant >= 0)[:, None]
    rank = jnp.sum(jnp.where(hit, prefix_count(hit) - 1, 0), axis=1)
    owner = jnp.where(tenant >= 0, position * OWN + rank, -1)
    owner_index = place(owner, slots, SLOTS)
    back_index = jnp.maximum(owner, 0)

    index = jnp.stack(
        [home_index, owner_index, back_index, jnp.pad(slot_of_row, (0, SLOTS - HOME))]
    )

    tenant_id = jnp.arange(client_device.shape[0], dtype=jnp.int32)
    here = client_device == x * TP + t
    first = jnp.min(jnp.where(here, tenant_id, client_device.shape[0]))
    second = jnp.max(jnp.where(here, tenant_id, -1))
    first_rank = jnp.sum(jnp.where(tenant_id == first, client_rank_bin, 0))
    second_rank = jnp.sum(jnp.where(tenant_id == second, client_rank_bin, 0))
    span = jnp.arange(rank_columns, dtype=jnp.int32)
    after = span >= first_rank
    gains = adapter_scale_fn / jnp.sqrt(jnp.stack([first_rank, second_rank]).astype(F32))
    gains = jnp.stack(
        [
            jnp.where(after, 0.0, gains[0]),
            jnp.where(after & (span < first_rank + second_rank), gains[1], 0.0),
            jnp.full(rank_columns, first + 1, F32),
            jnp.full(rank_columns, second + 1, F32),
        ]
    )
    return index.astype(jnp.int32), jnp.pad(gains, ((0, 4), (0, 0)))


def body(
    index,
    gains,
    marks,
    hidden,
    weight_in,
    down_in,
    down_tail,
    up_in,
    out,
    fin_hbm,
    slabs,
    rows,
    xrecv,
    weight,
    packed,
    group_first,
    group_second,
    owned,
    wide,
    down,
    up,
    home_in,
    parts,
    relay,
    second_out,
    second_in,
    own_sum,
    latents,
    local_sem,
    down_sem,
    up_sem,
    w_sem,
    x_send,
    x_recv,
    a_send,
    a_recv,
    t_send,
    t_recv,
    b_send,
    b_recv,
    c_send,
    c_recv,
    r_send,
    r_recv,
    s_send,
    s_recv,
):
    width = weight.shape[2]
    depth = weight.shape[1]
    half = width // 4
    x, t = lax.axis_index("dp"), lax.axis_index("tp")
    z, y, core, chip = t // 8, (t // 2) % 4, t % 2, t // 2

    def put_wide(at, value):
        for j in range(value.shape[1] // 128):
            wide[j, at, :] = value[:, j * 128 : (j + 1) * 128]

    def get_wide(at, columns=LANES):
        return jnp.concatenate([wide[j, at, :] for j in range(columns // 128)], axis=1)

    def remote(src, dst, send, recv, device):
        return pltpu.make_async_remote_copy(
            src_ref=src,
            dst_ref=dst,
            send_sem=send,
            recv_sem=recv,
            device_id=device,
            device_id_type=MESH,
        )

    barrier = pltpu.get_barrier_semaphore()

    @pl.loop(1, TP)
    def _(i):
        pl.semaphore_signal(barrier, inc=1, device_id=(x, (t + i) % TP), device_id_type=MESH)

    @pl.loop(1, RING)
    def _(i):
        pl.semaphore_signal(barrier, inc=1, device_id=((x + i) % RING, t), device_id_type=MESH)

    for s in range(TP):
        low = s * depth // 128 * 128
        cover = hidden[:, low : low + LANES + 128].astype(F32)
        cover = pltpu.roll(cover, (LANES + 128 + low - s * depth) % (LANES + 128), 1)
        slabs[s // 2, s % 2 * HOME : (s % 2 + 1) * HOME, :] = cover[:, :LANES].astype(BF16)

    pl.semaphore_wait(barrier, TP - 1 + RING - 1)

    def others(count, me, act):
        @pl.loop(1, count)
        def _(i):
            act((me + i) % count)

    def x_copy(peer, slot):
        return remote(
            slabs.at[peer], xrecv.at[slot], x_send.at[peer], x_recv.at[slot], (x, 2 * peer + core)
        )

    x_own = pltpu.make_async_copy(slabs.at[chip], xrecv.at[chip], local_sem.at[0])
    w_out = remote(weight_in, weight.at[core], w_sem.at[0], w_sem.at[1], (x, t + 1 - 2 * core))
    w_own = pltpu.make_async_copy(weight_in, weight.at[core], local_sem.at[1])

    def base_start():
        others(CHIPS, chip, lambda peer: x_copy(peer, chip).start())
        x_own.start()
        w_out.start()
        w_own.start()

    def base_arrived():
        w_own.wait()
        w_out.wait()
        x_own.wait()
        others(CHIPS, chip, lambda peer: x_copy(peer, peer).wait_recv())

    groups = (group_first, group_second)
    chunks = hidden.shape[1] // LANES

    def rows_ready():
        few = HOME // 2
        for k in range(2):
            own = slice(k * few, (k + 1) * few)

            @pl.loop(0, chunks)
            def _(c):
                put_wide(
                    pl.ds(c, few, stride=SLAB_ROWS),
                    hidden[own, pl.ds(pl.multiple_of(c * LANES, LANES), LANES)].astype(F32),
                )

            for c in range(chunks, SLAB_ROWS - 1):
                put_wide(pl.ds(c, few, stride=SLAB_ROWS), jnp.zeros((few, LANES), F32))
            for j in range(LANES // 128):
                wide[j, pl.ds(SLAB_ROWS - 1, few, stride=SLAB_ROWS), :] = marks[own, :]

            @pl.loop(0, few)
            def _(i):
                rows[k * few + i] = get_wide(pl.ds(i * SLAB_ROWS, SLAB_ROWS)).astype(BF16)

    def a_copy(h, peer, slot):
        return remote(
            packed.at[pl.ds(peer * CAP, CAP), pl.ds(h * PART, PART)],
            groups[h].at[pl.ds(slot * CAP, CAP)],
            a_send.at[h, peer],
            a_recv.at[h, slot],
            (peer, t),
        )

    def a_own(h):
        return pltpu.make_async_copy(
            packed.at[pl.ds(x * CAP, CAP), pl.ds(h * PART, PART)],
            groups[h].at[pl.ds(x * CAP, CAP)],
            local_sem.at[4 + h],
        )

    def group_start():
        @pl.loop(0, SLOTS)
        def _(i):
            packed[i] = rows[index[0, i]]

        for h in range(2):
            others(RING, x, lambda peer: a_copy(h, peer, x).start())
            a_own(h).start()

    def t_copy(h, peer, slot):
        return remote(
            packed.at[pl.ds(peer * OWN, OWN), pl.ds(h * PART, PART)],
            owned.at[pl.ds(slot * OWN, OWN), pl.ds(h * PART, PART)],
            t_send.at[h, peer],
            t_recv.at[h, slot],
            (x, peer),
        )

    def t_own(h):
        return pltpu.make_async_copy(
            packed.at[pl.ds(t * OWN, OWN), pl.ds(h * PART, PART)],
            owned.at[pl.ds(t * OWN, OWN), pl.ds(h * PART, PART)],
            local_sem.at[6 + h],
        )

    def owner_start(h):
        a_own(h).wait()
        others(RING, x, lambda peer: a_copy(h, peer, peer).wait_recv())
        others(RING, x, lambda peer: a_copy(h, peer, peer).wait_send())

        @pl.loop(0, SLOTS)
        def _(i):
            packed[i, h * PART : (h + 1) * PART, :] = groups[h][index[1, i]]

        others(TP, t, lambda peer: t_copy(h, peer, t).start())
        t_own(h).start()

    def axes(p):
        return (y, z) if p == 0 else (z, y)

    def device(p, a, b):
        return (x, (b * RING + a if p == 0 else a * RING + b) * 2 + core)

    def partial_sum(p, a_to, column):
        b = axes(p)[1]
        total = None
        for k in range(2):
            left = []
            for i in range(RING):
                b_to = (b + i) % RING
                at = b_to * RING + a_to if p == 0 else a_to * RING + b_to
                left.append(xrecv[at, k * HOME : (k + 1) * HOME, :][:, :depth])
            term = jnp.dot(
                jnp.concatenate(left, axis=0),
                weight[k, :, pl.ds(column, TILE)],
                preferred_element_type=F32,
            )
            total = term if total is None else total + term
        return total

    def fill(p, slot, a_to, side, added=None):
        @pl.loop(0, half // TILE)
        def _(n):
            col = pl.multiple_of(n * TILE, TILE)
            total = partial_sum(p, a_to, pl.multiple_of((2 * p + side) * half + n * TILE, TILE))
            if added is not None:
                total = total + relay[p, added, :, pl.ds(col, TILE)].astype(F32)
            parts[p, slot, :, pl.ds(col, TILE)] = total.astype(BF16)

    def r_copy(p, k):
        a, b = axes(p)
        up_to, down_to = device(p, (a + 1) % RING, b), device(p, (a + 3) % RING, b)
        src, dst, to = [
            (0, relay.at[p, 0], up_to),
            (1, relay.at[p, 1], down_to),
            (2, fin_hbm.at[p, 1], up_to),
            (3, fin_hbm.at[p, 2], down_to),
            (0, fin_hbm.at[p, 0], up_to),
            (1, fin_hbm.at[p, 3], down_to),
        ][k]
        return remote(parts.at[p, src], dst, r_send.at[p, k], r_recv.at[p, k], to)

    def reduce_far(p):
        for k in range(2):
            fill(p, k, (axes(p)[0] + 2) % RING, k)
            r_copy(p, k).start()

    def reduce_near(p):
        for k in range(2):
            fill(p, 2 + k, (axes(p)[0] + 1 + 2 * k) % RING, 1 - k)
            r_copy(p, 2 + k).start()

    def reduce_pass(p):
        for k in range(2):
            r_copy(p, k).wait()
            fill(p, k, (axes(p)[0] + 1 + 2 * k) % RING, k, added=k)
            r_copy(p, 4 + k).start()

    def down_copy(s):
        return pltpu.make_async_copy(
            down_in.at[:, pl.ds(pl.multiple_of(s * LANES, LANES), LANES)],
            down.at[s % AHEAD],
            down_sem.at[s % AHEAD],
        )

    def up_copy(s):
        return pltpu.make_async_copy(
            up_in.at[:, pl.ds(pl.multiple_of(s * TILE, TILE), TILE)],
            up.at[s % UP_AHEAD],
            up_sem.at[s % UP_AHEAD],
        )

    def factors_start():
        for s in range(AHEAD):
            down_copy(s).start()
        for s in range(UP_AHEAD):
            up_copy(s).start()

    def latent_part(h):
        t_own(h).wait()
        others(TP, t, lambda peer: t_copy(h, peer, peer).wait_recv())

        @pl.loop(0, SLOTS)
        def _(i):
            put_wide(
                pl.ds(i * PART, PART), owned[i, h * PART : (h + 1) * PART, :].astype(F32)
            )

        first, last = h * PART, min((h + 1) * PART, chunks)

        @pl.loop(0, last - first)
        def _(s):
            piece = get_wide(pl.ds(s, SLOTS, stride=PART)).astype(BF16)
            rows[pl.ds(s * OWN, OWN)] = piece.reshape(OWN, SLAB_ROWS, LANES)

        def term(s, factors):
            left = rows[pl.ds((s - first) * OWN, OWN)].reshape(SLOTS, LANES)
            return lax.dot_general(
                left, factors, (((1,), (1,)), ((), ())), preferred_element_type=F32
            )

        def step(s, total):
            down_copy(s).wait()
            total = total + term(s, down[s % AHEAD])

            @pl.when(s + AHEAD < chunks - 1)
            def _():
                down_copy(s + AHEAD).start()

            return total

        if h == 0:
            start = jnp.zeros(latents.shape, F32)
        else:
            start = latents[...] + term(chunks - 1, down_tail[...])
        total = lax.fori_loop(first, min(last, chunks - 1), step, start)
        if h == 1:
            mark = get_wide(pl.ds(PART - 1, SLOTS, stride=PART))[:, : latents.shape[1]]
            total = total * (
                jnp.where(mark == gains[2:3, :], gains[0:1, :], 0.0)
                + jnp.where(mark == gains[3:4, :], gains[1:2, :], 0.0)
            )
        latents[...] = total

    def b_copy(h, peer, slot):
        return remote(
            packed.at[pl.ds(peer * OWN, OWN), pl.ds(h * PART, PART), pl.ds(0, OUT)],
            groups[h].at[pl.ds(slot * OWN, OWN), :, pl.ds(0, OUT)],
            b_send.at[h, peer],
            b_recv.at[h, slot],
            (x, peer),
        )

    def b_own(h):
        return pltpu.make_async_copy(
            packed.at[pl.ds(t * OWN, OWN), pl.ds(h * PART, PART), pl.ds(0, OUT)],
            groups[h].at[pl.ds(t * OWN, OWN), :, pl.ds(0, OUT)],
            local_sem.at[8 + h],
        )

    def back_start(h):
        steps = up_in.shape[1] // TILE
        left = latents[...].astype(BF16)
        others(TP, t, lambda peer: t_copy(h, peer, peer).wait_send())

        @pl.loop(h * steps // 2, (h + 1) * steps // 2)
        def _(s):
            up_copy(s).wait()
            product = jnp.dot(left, up[s % UP_AHEAD], preferred_element_type=F32)
            for j in range(TILE // OUT):
                put_wide(
                    pl.ds((s - h * (steps // 2)) * (TILE // OUT) + j, SLOTS, stride=PART),
                    product[:, j * OUT : (j + 1) * OUT],
                )

            @pl.when(s + UP_AHEAD < steps)
            def _():
                up_copy(s + UP_AHEAD).start()

        @pl.loop(0, SLOTS)
        def _(i):
            packed[i, h * PART : (h + 1) * PART, :OUT] = get_wide(
                pl.ds(i * PART, PART), OUT
            ).astype(BF16)

        others(TP, t, lambda peer: b_copy(h, peer, t).start())
        b_own(h).start()

    def s_copy(p, d):
        a, b = axes(p)
        return remote(
            second_out.at[p, d - 1],
            second_in.at[p, d - 1],
            s_send.at[p, d - 1],
            s_recv.at[p, d - 1],
            device(p, a, (b + d) % RING),
        )

    def reduce_second(p):
        for k in range(2, 6):
            r_copy(p, k).wait()
        fin = pltpu.make_async_copy(fin_hbm.at[p], parts.at[p], local_sem.at[2 + p])
        fin.start()
        fin.wait()
        for side in range(2):

            @pl.loop(0, half // TILE)
            def _(n):
                col = pl.multiple_of(n * TILE, TILE)
                at = pl.multiple_of(side * half + n * TILE, TILE)
                total = partial_sum(
                    p, axes(p)[0], pl.multiple_of((2 * p + side) * half + n * TILE, TILE)
                )
                total = total + parts[p, side, :, pl.ds(col, TILE)].astype(F32)
                total = total + parts[p, 2 + side, :, pl.ds(col, TILE)].astype(F32)
                own_sum[p, :, pl.ds(at, TILE)] = total[:HOME]
                for d in range(1, RING):
                    second_out[p, d - 1, :, pl.ds(at, TILE)] = total[
                        d * HOME : (d + 1) * HOME
                    ].astype(BF16)

        for d in range(1, RING):
            s_copy(p, d).start()

    def c_copy(h, peer, slot):
        return remote(
            packed.at[pl.ds(peer * CAP, CAP), pl.ds(h * PART, PART), pl.ds(OUT, OUT)],
            home_in.at[pl.ds(slot * CAP, CAP), pl.ds(h * PART, PART)],
            c_send.at[h, peer],
            c_recv.at[h, slot],
            (peer, t),
        )

    def c_own(h):
        return pltpu.make_async_copy(
            packed.at[pl.ds(x * CAP, CAP), pl.ds(h * PART, PART), pl.ds(OUT, OUT)],
            home_in.at[pl.ds(x * CAP, CAP), pl.ds(h * PART, PART)],
            local_sem.at[10 + h],
        )

    def home_start(h):
        b_own(h).wait()
        others(TP, t, lambda peer: b_copy(h, peer, peer).wait_recv())

        @pl.loop(0, SLOTS)
        def _(i):
            packed[i, h * PART : (h + 1) * PART, OUT:] = groups[h][index[2, i]][:, :OUT]

        others(RING, x, lambda peer: c_copy(h, peer, x).start())
        c_own(h).start()

    def second_arrived():
        for p in range(2):
            for d in range(1, RING):
                s_copy(p, d).wait()

    def home_arrived(h):
        c_own(h).wait()
        others(RING, x, lambda peer: c_copy(h, peer, peer).wait_recv())

    def finish():
        few = HOME // 2
        for k in range(2):
            own = slice(k * few, (k + 1) * few)

            @pl.loop(0, few)
            def _(i):
                put_wide(pl.ds(i * SLAB_ROWS, SLAB_ROWS), home_in[index[3, k * few + i]].astype(F32))

            for p in range(2):

                @pl.loop(0, PART)
                def _(n):
                    at = pl.ds(pl.multiple_of(n * OUT, OUT), OUT)
                    total = own_sum[p, own, at]
                    for d in range(3):
                        total = total + second_in[p, d, own, at].astype(F32)
                    total = total + get_wide(pl.ds(p * PART + n, few, stride=SLAB_ROWS), OUT)
                    column = pl.multiple_of(p * 2 * half + n * OUT, OUT)
                    out[own, pl.ds(column, OUT)] = total.astype(BF16)

    def all_left():
        others(CHIPS, chip, lambda peer: x_copy(peer, peer).wait_send())
        for h in range(2):
            others(TP, t, lambda peer: b_copy(h, peer, peer).wait_send())
            others(RING, x, lambda peer: c_copy(h, peer, peer).wait_send())

    base_start()
    factors_start()
    rows_ready()
    group_start()
    owner_start(0)
    base_arrived()
    reduce_far(0)
    owner_start(1)
    reduce_far(1)
    reduce_near(0)
    reduce_near(1)
    latent_part(0)
    reduce_pass(0)
    reduce_pass(1)
    latent_part(1)
    back_start(0)
    back_start(1)
    reduce_second(0)
    home_start(0)
    reduce_second(1)
    home_start(1)
    second_arrived()
    home_arrived(0)
    home_arrived(1)
    finish()
    all_left()


def local(
    hidden,
    draft_row_client,
    client_rank_bin,
    client_device,
    down_weight,
    packed_down_factors,
    packed_up_factors,
):
    depth, width = down_weight.shape
    rank_columns = packed_down_factors.shape[1]
    index, gains = routing(draft_row_client, client_rank_bin, client_device, rank_columns)
    units = hidden.shape[1]
    padded = -(-units // LANES) * LANES
    marks = jnp.broadcast_to((draft_row_client + 1).astype(F32)[:, None], (HOME, 128))
    rows = jnp.pad(hidden, ((0, 0), (0, padded - units)))
    down = packed_down_factors.T
    tail = units // LANES * LANES
    down_tail = jnp.pad(down[:, tail:], ((0, 0), (0, LANES - units + tail)))

    vmem, hbm = pl.BlockSpec(memory_space=pltpu.VMEM), pl.BlockSpec(memory_space=pl.ANY)
    dma = pltpu.SemaphoreType.DMA
    half = width // 4
    out, _ = pl.pallas_call(
        body,
        out_shape=(
            jax.ShapeDtypeStruct((HOME, width), BF16),
            jax.ShapeDtypeStruct((2, 4, RING * HOME, half), BF16),
        ),
        in_specs=[pl.BlockSpec(memory_space=pltpu.SMEM), vmem, vmem, vmem, hbm, hbm, vmem, hbm],
        out_specs=(vmem, hbm),
        scratch_shapes=[
            pltpu.VMEM((CHIPS, 2 * HOME, LANES), BF16),
            pltpu.VMEM((HOME, SLAB_ROWS, LANES), BF16),
            pltpu.VMEM((CHIPS, 2 * HOME, LANES), BF16),
            pltpu.VMEM((2, depth, width), BF16),
            pltpu.VMEM((SLOTS, SLAB_ROWS, LANES), BF16),
            pltpu.VMEM((SLOTS, PART, LANES), BF16),
            pltpu.VMEM((SLOTS, PART, LANES), BF16),
            pltpu.VMEM((SLOTS, SLAB_ROWS, LANES), BF16),
            pltpu.VMEM((LANES // 128, SLOTS * PART, 128), F32),
            pltpu.VMEM((AHEAD, rank_columns, LANES), BF16),
            pltpu.VMEM((UP_AHEAD, rank_columns, TILE), BF16),
            pltpu.VMEM((SLOTS, SLAB_ROWS, OUT), BF16),
            pltpu.VMEM((2, 4, RING * HOME, half), BF16),
            pltpu.VMEM((2, 2, RING * HOME, half), BF16),
            pltpu.VMEM((2, 3, HOME, 2 * half), BF16),
            pltpu.VMEM((2, 3, HOME, 2 * half), BF16),
            pltpu.VMEM((2, HOME, 2 * half), F32),
            pltpu.VMEM((SLOTS, rank_columns), F32),
            dma((12,)),
            dma((AHEAD,)),
            dma((UP_AHEAD,)),
            dma((2,)),
            dma((CHIPS,)),
            dma((CHIPS,)),
            dma((2, RING)),
            dma((2, RING)),
            dma((2, TP)),
            dma((2, TP)),
            dma((2, TP)),
            dma((2, TP)),
            dma((2, RING)),
            dma((2, RING)),
            dma((2, 6)),
            dma((2, 6)),
            dma((2, 3)),
            dma((2, 3)),
        ],
        compiler_params=pltpu.CompilerParams(
            collective_id=0, has_side_effects=True, vmem_limit_bytes=63 << 20
        ),
        name="verify_rows",
    )(index, gains, marks, rows, down_weight, down, down_tail, packed_up_factors)
    return out


def solution(mesh):
    placed = (
        P(("dp", "tp"), None),
        P(("dp", "tp")),
        P(),
        P(),
        P("tp", None),
        P(None, ("dp", "tp")),
        P(("dp", "tp"), None),
    )
    return jax.shard_map(
        local, mesh=mesh, in_specs=placed, out_specs=P(("dp", "tp"), None), check_vma=False
    )
```

time: 261 us -> 227 us (0.87)
  the two profiles are of different devices: /device:TPU:25 before, /device:TPU:0 now
where the time goes in v3:
time: 227 us; the launch traced here: 225 us
  Pallas kernels  197 us (87%)
  other arithmetic  10.6 us (5%)
  local copies, waits for them, and re-layouts  9.94 us (4%)
  starting transfers between devices  4.38 us (2%)
  between operations  2.62 us (1%)
    pallas_call x1, Pallas kernels, local(): pl.pallas_call(body, out_shape=(jax.ShapeDtypeStruct((HOME, width), BF16)...  197 us
  transfers between devices with their start and end apart: 1, of which 0 were waited for; matrix products, arithmetic and copies ran while one was open for 6% of the time, Pallas kernels for 0%

profile of v3, /device:TPU:0, one launch (start us, length us, event | category | flops | bytes accessed | tf_op | source)
XLA Modules:
  0.0 224.5 jit_solution(11629409723733642373)
XLA Ops:
  0.0 0.9 select_reduce_fusion.1
  0.9 0.1 fusion.5
  1.0 0.7 fusion.21
  1.7 0.1 select_reduce_fusion.4
  1.8 0.7 all_to_all.6
  2.5 4.4 %all-to-all-start = ((s32[4,1,24]{2,1,0:T(1,128)}), s32[4,1,24]{2,1,0:T(1,128)S(1)}, u32[]{:S(2)}, u32[]{:S(2)}) async-start(s32[4,1,24]{2,1,0:T(1,128)} %bitcast.1), calls=%async_computation | async-start | bytes 4096 | tf_op jit(solution)/shard_map/all_to_all | solution.py:53
  6.9 1.4 select_reduce_fusion.6
  9.7 2.7 %fusion.10 = (s32[]{:T(128)}, s32[]{:T(128)}) fusion(s32[256]{0:T(256)} %param.9, s32[]{:T(128)} %get-tuple-element.9, s32[]{:T(128)} %get-tuple-element.10), kind=kLoop, calls=%fused_computation.42 | loop fusion | flops 1534 | bytes 1040 | tf_op jit(solution)/shard_map/reduce_sum | solution.py:79
  13.6 1.3 fusion.19
  14.9 0.7 fusion.22
  15.6 1.0 slice.12
  16.6 1.9 and_select_fusion
  18.5 0.8 pad.19.down_tail
  19.3 3.0 %pad.18.hidden = bf16[64,14848]{1,0:T(8,128)(2,1)} pad(bf16[64,14784]{1,0:T(8,128)(2,1)} %param.7, bf16[]{:T(256)} %constant.66.clone.1), padding=0_0x0_64 | pad | bytes 3792898 | tf_op jit(solution)/shard_map/jit(_pad)/pad | solution.py:600
  22.3 0.6 pad.17.gains
  22.9 0.1 sub.23
  23.0 0.9 select_reduce_fusion
  23.9 0.1 ge.42
  24.0 0.2 fusion.2
  24.2 0.1 select_reduce_fusion.2
  24.3 0.6 pad_add_fusion.index
  24.9 0.7 broadcast_in_dim.133.marks
  25.6 196.7 %verify_rows.1 = (bf16[64,8192]{1,0:T(8,128)(2,1)}, bf16[2,4,256,2048]{3,2,1,0:T(8,128)(2,1)}) custom-call(s32[4,96]{1,0:T(4,128)} %pad_add_fusion.index, f32[8,320]{1,0:T(8,128)} %pad.17.gains, f32[64,128]{1,0:T(8,128)} %broadcast_in_dim.133.marks, bf16[64,14848]{1,0:T(8,128)(2,1)} %pad.18.hidden, bf16[462,8192]{1,0:T(8,128)(2,1)} %weight_in.1, ...), custom_call_target="tpu_custom_call" | custom-call | tf_op jit(solution)/shard_map/verify_rows/pallas_call | solution.py:608
  222.3 2.3 %copy.12 = bf16[64,8192]{1,0:T(8,128)(2,1)} copy(bf16[64,8192]{1,0:T(8,128)(2,1)} %get-tuple-element.6) | data formatting | bytes 2097152
  (12 shorter events, 0.3 us)
Async XLA Ops:
  2.5 20.4 %all-to-all-start = ((s32[4,1,24]{2,1,0:T(1,128)}), s32[4,1,24]{2,1,0:T(1,128)S(1)}, u32[]{:S(2)}, u32[]{:S(2)}) async-start(s32[4,1,24]{2,1,0:T(1,128)} %bitcast.1), calls=%async_computation | async-start | bytes 4096 | tf_op jit(solution)/shard_map/all_to_all | solution.py:53

commit v4 on v3

--- a/solution.py
+++ b/solution.py
@@ -28,49 +28,11 @@
 UP_AHEAD = 4
 
 
-def prefix_count(match):
-    n = match.shape[0]
-    order = jnp.arange(n, dtype=jnp.int32)
-    tri = (order[None, :] <= order[:, None]).astype(BF16)
-    return jnp.dot(tri, match.astype(BF16), preferred_element_type=F32).astype(jnp.int32)
-
-
-def lookup(index, table):
-    hit = index[:, None] == jnp.arange(table.shape[0], dtype=jnp.int32)[None, :]
-    return jnp.sum(jnp.where(hit, table[None, :], 0), axis=1)
-
-
-def place(target, value, size):
-    hit = jnp.arange(size, dtype=jnp.int32)[:, None] == target[None, :]
-    return jnp.sum(jnp.where(hit, value[None, :], 0), axis=1)
-
-
-def routing(draft_row_client, client_rank_bin, client_device, rank_columns):
+def tables(client_rank_bin, client_device, rank_columns):
     x, t = lax.axis_index("dp"), lax.axis_index("tp")
-    slots = jnp.arange(SLOTS, dtype=jnp.int32)
-
-    def send(values, axis, parts):
-        return lax.all_to_all(
-            values.reshape(parts, SLOTS // parts), axis, split_axis=0, concat_axis=0, tiled=True
-        ).reshape(SLOTS)
-
-    group = lookup(draft_row_client, client_device) // TP
-    hit = group[:, None] == jnp.arange(RING, dtype=jnp.int32)[None, :]
-    rank = jnp.sum(jnp.where(hit, prefix_count(hit) - 1, 0), axis=1)
-    slot_of_row = group * CAP + rank
-    home_index = place(slot_of_row, jnp.arange(HOME, dtype=jnp.int32), SLOTS)
-
-    tenant = send(place(slot_of_row, draft_row_client + 1, SLOTS), "dp", RING) - 1
-    position = lookup(tenant, client_device) % TP
-    hit = (position[:, None] == jnp.arange(TP, dtype=jnp.int32)[None, :]) & (tenant >= 0)[:, None]
-    rank = jnp.sum(jnp.where(hit, prefix_count(hit) - 1, 0), axis=1)
-    owner = jnp.where(tenant >= 0, position * OWN + rank, -1)
-    owner_index = place(owner, slots, SLOTS)
-    back_index = jnp.maximum(owner, 0)
-
-    index = jnp.stack(
-        [home_index, owner_index, back_index, jnp.pad(slot_of_row, (0, SLOTS - HOME))]
-    )
+    column = jnp.arange(128, dtype=jnp.int32)[None, :]
+    device = client_device[:, None]
+    places = ((column < TP) & (device == x * TP + column)) | (column == TP + device // TP)
 
     tenant_id = jnp.arange(client_device.shape[0], dtype=jnp.int32)
     here = client_device == x * TP + t
@@ -78,22 +40,20 @@
     second = jnp.max(jnp.where(here, tenant_id, -1))
     first_rank = jnp.sum(jnp.where(tenant_id == first, client_rank_bin, 0))
     second_rank = jnp.sum(jnp.where(tenant_id == second, client_rank_bin, 0))
-    span = jnp.arange(rank_columns, dtype=jnp.int32)
+    span = jnp.arange(rank_columns, dtype=jnp.int32)[None, :]
+    kind = jnp.arange(8, dtype=jnp.int32)[:, None]
     after = span >= first_rank
-    gains = adapter_scale_fn / jnp.sqrt(jnp.stack([first_rank, second_rank]).astype(F32))
-    gains = jnp.stack(
-        [
-            jnp.where(after, 0.0, gains[0]),
-            jnp.where(after & (span < first_rank + second_rank), gains[1], 0.0),
-            jnp.full(rank_columns, first + 1, F32),
-            jnp.full(rank_columns, second + 1, F32),
-        ]
+    gain = adapter_scale_fn / jnp.sqrt(
+        jnp.where(kind == 0, first_rank, second_rank).astype(F32)
     )
-    return index.astype(jnp.int32), jnp.pad(gains, ((0, 4), (0, 0)))
+    inside = jnp.where(kind == 0, ~after, after & (span < first_rank + second_rank))
+    marks = jnp.where(kind == 2, first + 1, second + 1).astype(F32)
+    gains = jnp.where(kind < 2, jnp.where(inside, gain, 0.0), marks)
+    return places.astype(BF16), gains
 
 
 def body(
-    index,
+    places,
     gains,
     marks,
     hidden,
@@ -121,6 +81,9 @@
     second_in,
     own_sum,
     latents,
+    gain,
+    found,
+    index,
     local_sem,
     down_sem,
     up_sem,
@@ -207,6 +170,48 @@
         x_own.wait()
         others(CHIPS, chip, lambda peer: x_copy(peer, peer).wait_recv())
 
+    def running(hit):
+        n = hit.shape[0]
+        order = lax.broadcasted_iota(jnp.int32, (n, n), 0) >= lax.broadcasted_iota(
+            jnp.int32, (n, n), 1
+        )
+        return jnp.dot(
+            order.astype(F32).astype(BF16), hit.astype(BF16), preferred_element_type=F32
+        )
+
+    def target(mark, low, count, capacity):
+        n = mark.shape[0]
+        column = lax.broadcasted_iota(jnp.int32, (n, 128), 1)
+        tenants = [(mark == (column + 1 + k).astype(F32)).astype(F32) for k in (0, 128)]
+        hit = jnp.dot(
+            jnp.concatenate(tenants, axis=1).astype(BF16), places[...], preferred_element_type=F32
+        )
+        hit = jnp.where((column >= low) & (column < low + count), hit, 0.0)
+        slot = (column - low).astype(F32) * capacity + running(hit) - 1.0
+        slot = jnp.sum(hit * slot, axis=1, keepdims=True)
+        return jnp.where(jnp.sum(hit, axis=1, keepdims=True) > 0, slot, -1.0)
+
+    def set_index(row, slot, empty):
+        n = slot.shape[0]
+        column = lax.broadcasted_iota(jnp.int32, (n, 128), 1)
+        source = lax.broadcasted_iota(jnp.int32, (n, 128), 0)
+        back = jnp.where(slot == column.astype(F32), (source - empty).astype(F32), 0.0)
+        forth = jnp.where(source == column, jnp.maximum(slot, 0.0), 0.0)
+        found[row] = jnp.broadcast_to(
+            jnp.sum(back, axis=0, keepdims=True).astype(jnp.int32) + empty, (8, 128)
+        )
+        found[row + 1] = jnp.broadcast_to(
+            jnp.sum(forth, axis=0, keepdims=True).astype(jnp.int32), (8, 128)
+        )
+        copy = pltpu.make_async_copy(
+            found.at[pl.ds(row, 2)], index.at[pl.ds(row, 2)], local_sem.at[12 + row // 2]
+        )
+        copy.start()
+        copy.wait()
+
+    def at_index(row, i, size):
+        return jnp.minimum(jnp.maximum(index[row, 0, i], 0), size - 1)
+
     groups = (group_first, group_second)
     chunks = hidden.shape[1] // LANES
 
@@ -215,21 +220,21 @@
         for k in range(2):
             own = slice(k * few, (k + 1) * few)
 
-            @pl.loop(0, chunks)
-            def _(c):
+            for c in range(chunks):
                 put_wide(
-                    pl.ds(c, few, stride=SLAB_ROWS),
-                    hidden[own, pl.ds(pl.multiple_of(c * LANES, LANES), LANES)].astype(F32),
+                    pl.ds(c + c // (PART - 1), few, stride=SLAB_ROWS),
+                    hidden[own, c * LANES : (c + 1) * LANES].astype(F32),
                 )
-
-            for c in range(chunks, SLAB_ROWS - 1):
+            for c in range(chunks + 1, SLAB_ROWS):
                 put_wide(pl.ds(c, few, stride=SLAB_ROWS), jnp.zeros((few, LANES), F32))
             for j in range(LANES // 128):
-                wide[j, pl.ds(SLAB_ROWS - 1, few, stride=SLAB_ROWS), :] = marks[own, :]
+                wide[j, pl.ds(PART - 1, few, stride=SLAB_ROWS), :] = marks[own, :]
 
             @pl.loop(0, few)
             def _(i):
                 rows[k * few + i] = get_wide(pl.ds(i * SLAB_ROWS, SLAB_ROWS)).astype(BF16)
+
+        rows[HOME] = jnp.zeros(rows.shape[1:], BF16)
 
     def a_copy(h, peer, slot):
         return remote(
@@ -248,9 +253,11 @@
         )
 
     def group_start():
+        set_index(0, target(marks[...], TP, RING, CAP), HOME)
+
         @pl.loop(0, SLOTS)
         def _(i):
-            packed[i] = rows[index[0, i]]
+            packed[i] = rows[at_index(0, i, HOME + 1)]
 
         for h in range(2):
             others(RING, x, lambda peer: a_copy(h, peer, x).start())
@@ -277,9 +284,18 @@
         others(RING, x, lambda peer: a_copy(h, peer, peer).wait_recv())
         others(RING, x, lambda peer: a_copy(h, peer, peer).wait_send())
 
+        if h == 0:
+
+            @pl.loop(0, SLOTS)
+            def _(i):
+                wide[0, pl.ds(i * PART, PART), :] = groups[h][i, :, :128].astype(F32)
+
+            mark = wide[0, pl.ds(PART - 1, SLOTS, stride=PART), :]
+            set_index(2, target(mark, 0, TP, OWN), 0)
+
         @pl.loop(0, SLOTS)
         def _(i):
-            packed[i, h * PART : (h + 1) * PART, :] = groups[h][index[1, i]]
+            packed[i, h * PART : (h + 1) * PART, :] = groups[h][at_index(2, i, SLOTS)]
 
         others(TP, t, lambda peer: t_copy(h, peer, t).start())
         t_own(h).start()
@@ -375,7 +391,7 @@
                 pl.ds(i * PART, PART), owned[i, h * PART : (h + 1) * PART, :].astype(F32)
             )
 
-        first, last = h * PART, min((h + 1) * PART, chunks)
+        first, last = h * (PART - 1), PART - 1 if h == 0 else chunks
 
         @pl.loop(0, last - first)
         def _(s):
@@ -399,17 +415,17 @@
             return total
 
         if h == 0:
+            mark = get_wide(pl.ds(PART - 1, SLOTS, stride=PART))[:, : latents.shape[1]]
+            gain[...] = jnp.where(mark == gains[2:3, :], gains[0:1, :], 0.0) + jnp.where(
+                mark == gains[3:4, :], gains[1:2, :], 0.0
+            )
+
+        if h == 0:
             start = jnp.zeros(latents.shape, F32)
         else:
             start = latents[...] + term(chunks - 1, down_tail[...])
         total = lax.fori_loop(first, min(last, chunks - 1), step, start)
-        if h == 1:
-            mark = get_wide(pl.ds(PART - 1, SLOTS, stride=PART))[:, : latents.shape[1]]
-            total = total * (
-                jnp.where(mark == gains[2:3, :], gains[0:1, :], 0.0)
-                + jnp.where(mark == gains[3:4, :], gains[1:2, :], 0.0)
-            )
-        latents[...] = total
+        latents[...] = total if h == 0 else total * gain[...]
 
     def b_copy(h, peer, slot):
         return remote(
@@ -455,41 +471,51 @@
         others(TP, t, lambda peer: b_copy(h, peer, t).start())
         b_own(h).start()
 
-    def s_copy(p, d):
+    def s_copy(p, side, d):
         a, b = axes(p)
         return remote(
-            second_out.at[p, d - 1],
-            second_in.at[p, d - 1],
-            s_send.at[p, d - 1],
-            s_recv.at[p, d - 1],
+            second_out.at[p, side, d - 1],
+            second_in.at[p, side, d - 1],
+            s_send.at[p, side, d - 1],
+            s_recv.at[p, side, d - 1],
             device(p, a, (b + d) % RING),
         )
 
-    def reduce_second(p):
-        for k in range(2, 6):
-            r_copy(p, k).wait()
-        fin = pltpu.make_async_copy(fin_hbm.at[p], parts.at[p], local_sem.at[2 + p])
-        fin.start()
-        fin.wait()
-        for side in range(2):
-
-            @pl.loop(0, half // TILE)
-            def _(n):
-                col = pl.multiple_of(n * TILE, TILE)
-                at = pl.multiple_of(side * half + n * TILE, TILE)
-                total = partial_sum(
-                    p, axes(p)[0], pl.multiple_of((2 * p + side) * half + n * TILE, TILE)
+    def reduce_second(p, side):
+        came = (4, 3) if side == 0 else (2, 5)
+        stage = []
+        for i, k in enumerate(came):
+            r_copy(p, k).wait_recv()
+            slot = side + 2 * i
+            stage.append(
+                pltpu.make_async_copy(
+                    fin_hbm.at[p, slot], parts.at[p, slot], local_sem.at[16 + 4 * p + slot]
                 )
-                total = total + parts[p, side, :, pl.ds(col, TILE)].astype(F32)
-                total = total + parts[p, 2 + side, :, pl.ds(col, TILE)].astype(F32)
-                own_sum[p, :, pl.ds(at, TILE)] = total[:HOME]
-                for d in range(1, RING):
-                    second_out[p, d - 1, :, pl.ds(at, TILE)] = total[
-                        d * HOME : (d + 1) * HOME
-                    ].astype(BF16)
+            )
+        for k in (4 + side, 2 + side):
+            r_copy(p, k).wait_send()
+        for copy in stage:
+            copy.start()
+        for copy in stage:
+            copy.wait()
+
+        @pl.loop(0, half // TILE)
+        def _(n):
+            col = pl.multiple_of(n * TILE, TILE)
+            at = pl.multiple_of(side * half + n * TILE, TILE)
+            total = partial_sum(
+                p, axes(p)[0], pl.multiple_of((2 * p + side) * half + n * TILE, TILE)
+            )
+            total = total + parts[p, side, :, pl.ds(col, TILE)].astype(F32)
+            total = total + parts[p, 2 + side, :, pl.ds(col, TILE)].astype(F32)
+            own_sum[p, :, pl.ds(at, TILE)] = total[:HOME]
+            for d in range(1, RING):
+                second_out[p, side, d - 1, :, pl.ds(col, TILE)] = total[
+                    d * HOME : (d + 1) * HOME
+                ].astype(BF16)
 
         for d in range(1, RING):
-            s_copy(p, d).start()
+            s_copy(p, side, d).start()
 
     def c_copy(h, peer, slot):
         return remote(
@@ -513,15 +539,16 @@
 
         @pl.loop(0, SLOTS)
         def _(i):
-            packed[i, h * PART : (h + 1) * PART, OUT:] = groups[h][index[2, i]][:, :OUT]
+            packed[i, h * PART : (h + 1) * PART, OUT:] = groups[h][at_index(3, i, SLOTS)][:, :OUT]
 
         others(RING, x, lambda peer: c_copy(h, peer, x).start())
         c_own(h).start()
 
     def second_arrived():
         for p in range(2):
-            for d in range(1, RING):
-                s_copy(p, d).wait()
+            for side in range(2):
+                for d in range(1, RING):
+                    s_copy(p, side, d).wait()
 
     def home_arrived(h):
         c_own(h).wait()
@@ -534,19 +561,22 @@
 
             @pl.loop(0, few)
             def _(i):
-                put_wide(pl.ds(i * SLAB_ROWS, SLAB_ROWS), home_in[index[3, k * few + i]].astype(F32))
+                put_wide(pl.ds(i * SLAB_ROWS, SLAB_ROWS), home_in[at_index(1, k * few + i, SLOTS)].astype(F32))
 
             for p in range(2):
-
-                @pl.loop(0, PART)
-                def _(n):
-                    at = pl.ds(pl.multiple_of(n * OUT, OUT), OUT)
-                    total = own_sum[p, own, at]
-                    for d in range(3):
-                        total = total + second_in[p, d, own, at].astype(F32)
-                    total = total + get_wide(pl.ds(p * PART + n, few, stride=SLAB_ROWS), OUT)
-                    column = pl.multiple_of(p * 2 * half + n * OUT, OUT)
-                    out[own, pl.ds(column, OUT)] = total.astype(BF16)
+                for side in range(2):
+
+                    @pl.loop(0, PART // 2)
+                    def _(n):
+                        at = pl.ds(pl.multiple_of(n * OUT, OUT), OUT)
+                        column = pl.multiple_of(side * half + n * OUT, OUT)
+                        total = own_sum[p, own, pl.ds(column, OUT)]
+                        for d in range(3):
+                            total = total + second_in[p, side, d, own, at].astype(F32)
+                        place = p * PART + side * (PART // 2) + n
+                        total = total + get_wide(pl.ds(place, few, stride=SLAB_ROWS), OUT)
+                        column = pl.multiple_of((2 * p + side) * half + n * OUT, OUT)
+                        out[own, pl.ds(column, OUT)] = total.astype(BF16)
 
     def all_left():
         others(CHIPS, chip, lambda peer: x_copy(peer, peer).wait_send())
@@ -571,9 +601,11 @@
     latent_part(1)
     back_start(0)
     back_start(1)
-    reduce_second(0)
+    reduce_second(0, 0)
+    reduce_second(1, 0)
     home_start(0)
-    reduce_second(1)
+    reduce_second(0, 1)
+    reduce_second(1, 1)
     home_start(1)
     second_arrived()
     home_arrived(0)
@@ -593,7 +625,7 @@
 ):
     depth, width = down_weight.shape
     rank_columns = packed_down_factors.shape[1]
-    index, gains = routing(draft_row_client, client_rank_bin, client_device, rank_columns)
+    places, gains = tables(client_rank_bin, client_device, rank_columns)
     units = hidden.shape[1]
     padded = -(-units // LANES) * LANES
     marks = jnp.broadcast_to((draft_row_client + 1).astype(F32)[:, None], (HOME, 128))
@@ -611,11 +643,11 @@
             jax.ShapeDtypeStruct((HOME, width), BF16),
             jax.ShapeDtypeStruct((2, 4, RING * HOME, half), BF16),
         ),
-        in_specs=[pl.BlockSpec(memory_space=pltpu.SMEM), vmem, vmem, vmem, hbm, hbm, vmem, hbm],
+        in_specs=[vmem, vmem, vmem, vmem, hbm, hbm, vmem, hbm],
         out_specs=(vmem, hbm),
         scratch_shapes=[
             pltpu.VMEM((CHIPS, 2 * HOME, LANES), BF16),
-            pltpu.VMEM((HOME, SLAB_ROWS, LANES), BF16),
+            pltpu.VMEM((HOME + 1, SLAB_ROWS, LANES), BF16),
             pltpu.VMEM((CHIPS, 2 * HOME, LANES), BF16),
             pltpu.VMEM((2, depth, width), BF16),
             pltpu.VMEM((SLOTS, SLAB_ROWS, LANES), BF16),
@@ -628,11 +660,14 @@
             pltpu.VMEM((SLOTS, SLAB_ROWS, OUT), BF16),
             pltpu.VMEM((2, 4, RING * HOME, half), BF16),
             pltpu.VMEM((2, 2, RING * HOME, half), BF16),
-            pltpu.VMEM((2, 3, HOME, 2 * half), BF16),
-            pltpu.VMEM((2, 3, HOME, 2 * half), BF16),
+            pltpu.VMEM((2, 2, 3, HOME, half), BF16),
+            pltpu.VMEM((2, 2, 3, HOME, half), BF16),
             pltpu.VMEM((2, HOME, 2 * half), F32),
             pltpu.VMEM((SLOTS, rank_columns), F32),
-            dma((12,)),
+            pltpu.VMEM((SLOTS, rank_columns), F32),
+            pltpu.VMEM((4, 8, 128), jnp.int32),
+            pltpu.SMEM((4, 8, 128), jnp.int32),
+            dma((24,)),
             dma((AHEAD,)),
             dma((UP_AHEAD,)),
             dma((2,)),
@@ -648,14 +683,14 @@
             dma((2, RING)),
             dma((2, 6)),
             dma((2, 6)),
-            dma((2, 3)),
-            dma((2, 3)),
+            dma((2, 2, 3)),
+            dma((2, 2, 3)),
         ],
         compiler_params=pltpu.CompilerParams(
             collective_id=0, has_side_effects=True, vmem_limit_bytes=63 << 20
         ),
         name="verify_rows",
-    )(index, gains, marks, rows, down_weight, down, down_tail, packed_up_factors)
+    )(places, gains, marks, rows, down_weight, down, down_tail, packed_up_factors)
     return out
 
 

time: 227 us -> 213 us (0.938)
  starting transfers between devices: 4.38 us -> 0 us
  Pallas kernels: 197 us -> 193 us
    all_to_all x1 -> x0, starting transfers between devices: 4.38 us -> none  [send(): lax.all_to_all(values.reshape(parts, SLOTS // parts), axis, split_axis=0,...]
    pallas_call x1, Pallas kernels: 197 us -> 193 us  [local(): pl.pallas_call(body, out_shape=(jax.ShapeDtypeStruct((HOME, width), BF16)...]
    reduce_sum x5 -> x1, other arithmetic: 4.6 us -> 2.68 us  [tables(): first_rank = jnp.sum(jnp.where(tenant_id == first, client_rank_bin, 0))]
  transfers between devices with their start and end apart: 1 -> 0, of which waited for: 0 -> 0; matrix products, arithmetic and copies ran while one was open for 6% -> 0% of each run, Pallas kernels for 0% -> 0%
where the time goes in v4:
time: 213 us; the launch traced here: 212 us
  Pallas kernels  193 us (91%)
  other arithmetic  8.63 us (4%)
  local copies, waits for them, and re-layouts  7.68 us (4%)
  between operations  2.58 us (1%)
    pallas_call x1, Pallas kernels, local(): pl.pallas_call(body, out_shape=(jax.ShapeDtypeStruct((HOME, width), BF16)...  193 us

profile of v4, /device:TPU:0, one launch (start us, length us, event | category | flops | bytes accessed | tf_op | source)
XLA Modules:
  0.0 211.9 jit_solution(5489791709850088768)
XLA Ops:
  0.0 0.7 add_convert_fusion
  0.7 1.4 select_reduce_fusion.1
  3.4 2.7 %fusion.4 = (s32[]{:T(128)}, s32[]{:T(128)}) fusion(s32[256]{0:T(256)} %param.9, s32[]{:T(128)} %get-tuple-element.9, s32[]{:T(128)} %get-tuple-element.10), kind=kLoop, calls=%fused_computation.15 | loop fusion | flops 1534 | bytes 1040 | tf_op jit(solution)/shard_map/reduce_sum | solution.py:41
  7.3 1.2 rsqrt_multiply_fusion
  8.5 0.6 fusion.2
  9.1 0.7 select_select_fusion.gains
  9.8 0.7 broadcast_in_dim.95.marks
  10.4 1.4 fusion.1.places
  11.9 1.0 slice.4
  12.9 0.8 pad.9.down_tail
  13.6 3.0 %pad.8.hidden = bf16[64,14848]{1,0:T(8,128)(2,1)} pad(bf16[64,14784]{1,0:T(8,128)(2,1)} %param.7, bf16[]{:T(256)} %constant.46.clone.1), padding=0_0x0_64 | pad | bytes 3792898 | tf_op jit(solution)/shard_map/jit(_pad)/pad | solution.py:632
  16.6 193.0 %verify_rows.1 = (bf16[64,8192]{1,0:T(8,128)(2,1)}, bf16[2,4,256,2048]{3,2,1,0:T(8,128)(2,1)}) custom-call(bf16[256,128]{1,0:T(8,128)(2,1)} %fusion.1.places, f32[8,320]{1,0:T(8,128)} %select_select_fusion.gains, f32[64,128]{1,0:T(8,128)} %broadcast_in_dim.95.marks, bf16[64,14848]{1,0:T(8,128)(2,1)} %pad.8.hidden, bf16[462,8192]{1,0:T(8,128)(2,1)} %weight_in.1, ...), custom_call_target="tpu_custom_call" | custom-call | tf_op jit(solution)/shard_map/verify_rows/pallas_call | solution.py:640
  209.6 2.3 %copy.9 = bf16[64,8192]{1,0:T(8,128)(2,1)} copy(bf16[64,8192]{1,0:T(8,128)(2,1)} %get-tuple-element.6) | data formatting | bytes 2097152
  (4 shorter events, 0.0 us)

commit v5 on v4

--- a/solution.py
+++ b/solution.py
@@ -28,38 +28,13 @@
 UP_AHEAD = 4
 
 
-def tables(client_rank_bin, client_device, rank_columns):
-    x, t = lax.axis_index("dp"), lax.axis_index("tp")
-    column = jnp.arange(128, dtype=jnp.int32)[None, :]
-    device = client_device[:, None]
-    places = ((column < TP) & (device == x * TP + column)) | (column == TP + device // TP)
-
-    tenant_id = jnp.arange(client_device.shape[0], dtype=jnp.int32)
-    here = client_device == x * TP + t
-    first = jnp.min(jnp.where(here, tenant_id, client_device.shape[0]))
-    second = jnp.max(jnp.where(here, tenant_id, -1))
-    first_rank = jnp.sum(jnp.where(tenant_id == first, client_rank_bin, 0))
-    second_rank = jnp.sum(jnp.where(tenant_id == second, client_rank_bin, 0))
-    span = jnp.arange(rank_columns, dtype=jnp.int32)[None, :]
-    kind = jnp.arange(8, dtype=jnp.int32)[:, None]
-    after = span >= first_rank
-    gain = adapter_scale_fn / jnp.sqrt(
-        jnp.where(kind == 0, first_rank, second_rank).astype(F32)
-    )
-    inside = jnp.where(kind == 0, ~after, after & (span < first_rank + second_rank))
-    marks = jnp.where(kind == 2, first + 1, second + 1).astype(F32)
-    gains = jnp.where(kind < 2, jnp.where(inside, gain, 0.0), marks)
-    return places.astype(BF16), gains
-
-
 def body(
-    places,
-    gains,
-    marks,
+    tenants,
+    rank_bins,
+    devices,
     hidden,
     weight_in,
     down_in,
-    down_tail,
     up_in,
     out,
     fin_hbm,
@@ -73,6 +48,7 @@
     owned,
     wide,
     down,
+    down_tail,
     up,
     home_in,
     parts,
@@ -82,6 +58,8 @@
     own_sum,
     latents,
     gain,
+    places,
+    gains,
     found,
     index,
     local_sem,
@@ -136,9 +114,19 @@
     def _(i):
         pl.semaphore_signal(barrier, inc=1, device_id=((x + i) % RING, t), device_id_type=MESH)
 
+    units = hidden.shape[1]
+
+    def columns(own, low, count):
+        if low + count <= units:
+            return hidden[own, low : low + count].astype(F32)
+        rest = hidden[own, low:units].astype(F32)
+        return jnp.concatenate(
+            [rest, jnp.zeros((rest.shape[0], low + count - units), F32)], axis=1
+        )
+
     for s in range(TP):
         low = s * depth // 128 * 128
-        cover = hidden[:, low : low + LANES + 128].astype(F32)
+        cover = columns(slice(0, HOME), low, LANES + 128)
         cover = pltpu.roll(cover, (LANES + 128 + low - s * depth) % (LANES + 128), 1)
         slabs[s // 2, s % 2 * HOME : (s % 2 + 1) * HOME, :] = cover[:, :LANES].astype(BF16)
 
@@ -213,7 +201,41 @@
         return jnp.minimum(jnp.maximum(index[row, 0, i], 0), size - 1)
 
     groups = (group_first, group_second)
-    chunks = hidden.shape[1] // LANES
+    chunks = -(-units // LANES)
+
+    def marks(own):
+        return jnp.broadcast_to((tenants[own, :] + 1).astype(F32), (own.stop - own.start, 128))
+
+    def tables_ready():
+        device, rank = devices[...].astype(F32), rank_bins[...].astype(F32)
+        n = device.shape[1]
+        tenant = lax.broadcasted_iota(jnp.int32, (1, n), 1).astype(F32)
+        same = lax.broadcasted_iota(jnp.int32, (n, n), 0) == lax.broadcasted_iota(
+            jnp.int32, (n, n), 1
+        )
+        down_device = jnp.sum(jnp.where(same, device, 0.0), axis=1, keepdims=True)
+        column = lax.broadcasted_iota(jnp.int32, (n, 128), 1)
+        low = jnp.where(column < TP, x * TP + column, (column - TP) * TP).astype(F32)
+        span = jnp.where(column < TP, 1, TP).astype(F32)
+        places[...] = jnp.where(
+            (down_device >= low) & (down_device < low + span), 1.0, 0.0
+        ).astype(BF16)
+
+        here = device == (x * TP + t).astype(F32)
+        first = jnp.min(jnp.where(here, tenant, float(n)), axis=1, keepdims=True)
+        second = jnp.max(jnp.where(here, tenant, -1.0), axis=1, keepdims=True)
+        first_rank = jnp.sum(jnp.where(tenant == first, rank, 0.0), axis=1, keepdims=True)
+        second_rank = jnp.sum(jnp.where(tenant == second, rank, 0.0), axis=1, keepdims=True)
+        wide_shape = (1, gains.shape[1])
+        span = lax.broadcasted_iota(jnp.int32, wide_shape, 1).astype(F32)
+        gains[0:1, :] = jnp.where(span < first_rank, adapter_scale_fn / jnp.sqrt(first_rank), 0.0)
+        gains[1:2, :] = jnp.where(
+            (span >= first_rank) & (span < first_rank + second_rank),
+            adapter_scale_fn / jnp.sqrt(second_rank),
+            0.0,
+        )
+        gains[2:3, :] = jnp.broadcast_to(first + 1.0, wide_shape)
+        gains[3:4, :] = jnp.broadcast_to(second + 1.0, wide_shape)
 
     def rows_ready():
         few = HOME // 2
@@ -223,12 +245,12 @@
             for c in range(chunks):
                 put_wide(
                     pl.ds(c + c // (PART - 1), few, stride=SLAB_ROWS),
-                    hidden[own, c * LANES : (c + 1) * LANES].astype(F32),
+                    columns(own, c * LANES, LANES),
                 )
             for c in range(chunks + 1, SLAB_ROWS):
                 put_wide(pl.ds(c, few, stride=SLAB_ROWS), jnp.zeros((few, LANES), F32))
             for j in range(LANES // 128):
-                wide[j, pl.ds(PART - 1, few, stride=SLAB_ROWS), :] = marks[own, :]
+                wide[j, pl.ds(PART - 1, few, stride=SLAB_ROWS), :] = marks(own)
 
             @pl.loop(0, few)
             def _(i):
@@ -253,7 +275,7 @@
         )
 
     def group_start():
-        set_index(0, target(marks[...], TP, RING, CAP), HOME)
+        set_index(0, target(marks(slice(0, HOME)), TP, RING, CAP), HOME)
 
         @pl.loop(0, SLOTS)
         def _(i):
@@ -368,6 +390,11 @@
             down_sem.at[s % AHEAD],
         )
 
+    tail = (chunks - 1) * LANES
+    tail_copy = pltpu.make_async_copy(
+        down_in.at[:, tail:units], down_tail, local_sem.at[24]
+    )
+
     def up_copy(s):
         return pltpu.make_async_copy(
             up_in.at[:, pl.ds(pl.multiple_of(s * TILE, TILE), TILE)],
@@ -380,6 +407,7 @@
             down_copy(s).start()
         for s in range(UP_AHEAD):
             up_copy(s).start()
+        tail_copy.start()
 
     def latent_part(h):
         t_own(h).wait()
@@ -400,6 +428,7 @@
 
         def term(s, factors):
             left = rows[pl.ds((s - first) * OWN, OWN)].reshape(SLOTS, LANES)
+            left = left[:, : factors.shape[1]]
             return lax.dot_general(
                 left, factors, (((1,), (1,)), ((), ())), preferred_element_type=F32
             )
@@ -423,6 +452,7 @@
         if h == 0:
             start = jnp.zeros(latents.shape, F32)
         else:
+            tail_copy.wait()
             start = latents[...] + term(chunks - 1, down_tail[...])
         total = lax.fori_loop(first, min(last, chunks - 1), step, start)
         latents[...] = total if h == 0 else total * gain[...]
@@ -471,15 +501,23 @@
         others(TP, t, lambda peer: b_copy(h, peer, t).start())
         b_own(h).start()
 
-    def s_copy(p, side, d):
+    def s_copy(p, side, kind):
         a, b = axes(p)
+        src, forward = [(1, True), (2 - 2 * side, False), (2 * side, True)][kind]
+        step = 1 if forward == (side == 0) else 3
         return remote(
-            second_out.at[p, side, d - 1],
-            second_in.at[p, side, d - 1],
-            s_send.at[p, side, d - 1],
-            s_recv.at[p, side, d - 1],
-            device(p, a, (b + d) % RING),
-        )
+            second_out.at[p, side, src],
+            second_in.at[p, side, kind],
+            s_send.at[p, side, kind],
+            s_recv.at[p, side, kind],
+            device(p, a, (b + step) % RING),
+        )
+
+    def second_pass(p, side):
+        s_copy(p, side, 0).wait()
+        held = second_out.at[p, side, 2 * side]
+        held[...] = (held[...].astype(F32) + second_in[p, side, 0].astype(F32)).astype(BF16)
+        s_copy(p, side, 2).start()
 
     def reduce_second(p, side):
         came = (4, 3) if side == 0 else (2, 5)
@@ -514,8 +552,8 @@
                     d * HOME : (d + 1) * HOME
                 ].astype(BF16)
 
-        for d in range(1, RING):
-            s_copy(p, side, d).start()
+        for kind in range(2):
+            s_copy(p, side, kind).start()
 
     def c_copy(h, peer, slot):
         return remote(
@@ -547,8 +585,8 @@
     def second_arrived():
         for p in range(2):
             for side in range(2):
-                for d in range(1, RING):
-                    s_copy(p, side, d).wait()
+                for kind in range(1, 3):
+                    s_copy(p, side, kind).wait()
 
     def home_arrived(h):
         c_own(h).wait()
@@ -571,8 +609,8 @@
                         at = pl.ds(pl.multiple_of(n * OUT, OUT), OUT)
                         column = pl.multiple_of(side * half + n * OUT, OUT)
                         total = own_sum[p, own, pl.ds(column, OUT)]
-                        for d in range(3):
-                            total = total + second_in[p, side, d, own, at].astype(F32)
+                        for kind in range(1, 3):
+                            total = total + second_in[p, side, kind, own, at].astype(F32)
                         place = p * PART + side * (PART // 2) + n
                         total = total + get_wide(pl.ds(place, few, stride=SLAB_ROWS), OUT)
                         column = pl.multiple_of((2 * p + side) * half + n * OUT, OUT)
@@ -586,6 +624,7 @@
 
     base_start()
     factors_start()
+    tables_ready()
     rows_ready()
     group_start()
     owner_start(0)
@@ -606,7 +645,11 @@
     home_start(0)
     reduce_second(0, 1)
     reduce_second(1, 1)
+    second_pass(0, 0)
+    second_pass(1, 0)
     home_start(1)
+    second_pass(0, 1)
+    second_pass(1, 1)
     second_arrived()
     home_arrived(0)
     home_arrived(1)
@@ -624,15 +667,8 @@
     packed_up_factors,
 ):
     depth, width = down_weight.shape
-    rank_columns = packed_down_factors.shape[1]
-    places, gains = tables(client_rank_bin, client_device, rank_columns)
-    units = hidden.shape[1]
-    padded = -(-units // LANES) * LANES
-    marks = jnp.broadcast_to((draft_row_client + 1).astype(F32)[:, None], (HOME, 128))
-    rows = jnp.pad(hidden, ((0, 0), (0, padded - units)))
-    down = packed_down_factors.T
-    tail = units // LANES * LANES
-    down_tail = jnp.pad(down[:, tail:], ((0, 0), (0, LANES - units + tail)))
+    units, rank_columns = packed_down_factors.shape
+    tenants = client_rank_bin.shape[0]
 
     vmem, hbm = pl.BlockSpec(memory_space=pltpu.VMEM), pl.BlockSpec(memory_space=pl.ANY)
     dma = pltpu.SemaphoreType.DMA
@@ -643,7 +679,7 @@
             jax.ShapeDtypeStruct((HOME, width), BF16),
             jax.ShapeDtypeStruct((2, 4, RING * HOME, half), BF16),
         ),
-        in_specs=[vmem, vmem, vmem, vmem, hbm, hbm, vmem, hbm],
+        in_specs=[vmem, vmem, vmem, vmem, hbm, hbm, hbm],
         out_specs=(vmem, hbm),
         scratch_shapes=[
             pltpu.VMEM((CHIPS, 2 * HOME, LANES), BF16),
@@ -656,6 +692,7 @@
             pltpu.VMEM((SLOTS, SLAB_ROWS, LANES), BF16),
             pltpu.VMEM((LANES // 128, SLOTS * PART, 128), F32),
             pltpu.VMEM((AHEAD, rank_columns, LANES), BF16),
+            pltpu.VMEM((rank_columns, units % LANES), BF16),
             pltpu.VMEM((UP_AHEAD, rank_columns, TILE), BF16),
             pltpu.VMEM((SLOTS, SLAB_ROWS, OUT), BF16),
             pltpu.VMEM((2, 4, RING * HOME, half), BF16),
@@ -665,9 +702,11 @@
             pltpu.VMEM((2, HOME, 2 * half), F32),
             pltpu.VMEM((SLOTS, rank_columns), F32),
             pltpu.VMEM((SLOTS, rank_columns), F32),
+            pltpu.VMEM((tenants, 128), BF16),
+            pltpu.VMEM((8, rank_columns), F32),
             pltpu.VMEM((4, 8, 128), jnp.int32),
             pltpu.SMEM((4, 8, 128), jnp.int32),
-            dma((24,)),
+            dma((25,)),
             dma((AHEAD,)),
             dma((UP_AHEAD,)),
             dma((2,)),
@@ -690,7 +729,15 @@
             collective_id=0, has_side_effects=True, vmem_limit_bytes=63 << 20
         ),
         name="verify_rows",
-    )(places, gains, marks, rows, down_weight, down, down_tail, packed_up_factors)
+    )(
+        draft_row_client.reshape(HOME, 1),
+        client_rank_bin.reshape(1, tenants),
+        client_device.reshape(1, tenants),
+        hidden,
+        down_weight,
+        packed_down_factors.T,
+        packed_up_factors,
+    )
     return out
 
 

time: 213 us -> 193 us (0.906)
  other arithmetic: 8.63 us -> 0 us
  Pallas kernels: 193 us -> 188 us
  local copies, waits for them, and re-layouts: 7.68 us -> 3.62 us
  between operations: 2.58 us -> 0.01 us
    pallas_call x1, Pallas kernels: 193 us -> 188 us  [local(): pl.pallas_call(body, out_shape=(jax.ShapeDtypeStruct((HOME, width), BF16)...]
    pad x2 -> x0, local copies, waits for them, and re-layouts: 3.75 us -> none  [the longest x1 2.99 us: local(): rows = jnp.pad(hidden, ((0, 0), (0, padded - units)))]
    reduce_sum x1 -> x0, other arithmetic: 2.68 us -> none  [tables(): first_rank = jnp.sum(jnp.where(tenant_id == first, client_rank_bin, 0))]
where the time goes in v5:
time: 193 us; the launch traced here: 192 us
  Pallas kernels  188 us (97%)
  local copies, waits for them, and re-layouts  3.62 us (2%)
    pallas_call x1, Pallas kernels, local(): pl.pallas_call(body, out_shape=(jax.ShapeDtypeStruct((HOME, width), BF16)...  188 us

profile of v5, /device:TPU:0, one launch (start us, length us, event | category | flops | bytes accessed | tf_op | source)
XLA Modules:
  0.0 192.1 jit_solution(10090364043112068940)
XLA Ops:
  0.0 1.4 copy.8.tenants
  1.4 188.5 %verify_rows.1 = (bf16[64,8192]{1,0:T(8,128)(2,1)}, bf16[2,4,256,2048]{3,2,1,0:T(8,128)(2,1)}) custom-call(s32[64,1]{1,0:T(8,128)} %copy.8.tenants, s32[1,256]{1,0:T(1,128)} %bitcast.5, s32[1,256]{1,0:T(1,128)} %bitcast.6, bf16[64,14784]{1,0:T(8,128)(2,1)} %hidden.1, bf16[462,8192]{1,0:T(8,128)(2,1)} %weight_in.1, bf16[320,14784]{1,0:T(8,128)(2,1)} %bitcast.4, ...), custom_call_target="tpu_custom_call" | custom-call | tf_op jit(solution)/shard_map/verify_rows/pallas_call | solution.py:676
  189.8 2.3 %copy.10 = bf16[64,8192]{1,0:T(8,128)(2,1)} copy(bf16[64,8192]{1,0:T(8,128)(2,1)} %get-tuple-element.6) | data formatting | bytes 2097152

commit v6 on v5

--- a/solution.py
+++ b/solution.py
@@ -204,7 +204,12 @@
     chunks = -(-units // LANES)
 
     def marks(own):
-        return jnp.broadcast_to((tenants[own, :] + 1).astype(F32), (own.stop - own.start, 128))
+        few = own.stop - own.start
+        row = jnp.broadcast_to((tenants[...] + 1).astype(F32), (few, HOME))
+        same = lax.broadcasted_iota(jnp.int32, (few, HOME), 0) + own.start
+        same = same == lax.broadcasted_iota(jnp.int32, (few, HOME), 1)
+        column = jnp.sum(jnp.where(same, row, 0.0), axis=1, keepdims=True)
+        return jnp.broadcast_to(column, (few, 128))
 
     def tables_ready():
         device, rank = devices[...].astype(F32), rank_bins[...].astype(F32)
@@ -367,21 +372,18 @@
         ][k]
         return remote(parts.at[p, src], dst, r_send.at[p, k], r_recv.at[p, k], to)
 
-    def reduce_far(p):
-        for k in range(2):
-            fill(p, k, (axes(p)[0] + 2) % RING, k)
-            r_copy(p, k).start()
-
-    def reduce_near(p):
-        for k in range(2):
-            fill(p, 2 + k, (axes(p)[0] + 1 + 2 * k) % RING, 1 - k)
-            r_copy(p, 2 + k).start()
-
-    def reduce_pass(p):
-        for k in range(2):
-            r_copy(p, k).wait()
-            fill(p, k, (axes(p)[0] + 1 + 2 * k) % RING, k, added=k)
-            r_copy(p, 4 + k).start()
+    def reduce_far(p, k):
+        fill(p, k, (axes(p)[0] + 2) % RING, k)
+        r_copy(p, k).start()
+
+    def reduce_near(p, k):
+        fill(p, 2 + k, (axes(p)[0] + 1 + 2 * k) % RING, 1 - k)
+        r_copy(p, 2 + k).start()
+
+    def reduce_pass(p, k):
+        r_copy(p, k).wait()
+        fill(p, k, (axes(p)[0] + 1 + 2 * k) % RING, k, added=k)
+        r_copy(p, 4 + k).start()
 
     def down_copy(s):
         return pltpu.make_async_copy(
@@ -588,6 +590,15 @@
                 for kind in range(1, 3):
                     s_copy(p, side, kind).wait()
 
+                @pl.loop(0, half // TILE)
+                def _(n):
+                    at = pl.ds(pl.multiple_of(n * TILE, TILE), TILE)
+                    column = pl.ds(pl.multiple_of(side * half + n * TILE, TILE), TILE)
+                    total = own_sum[p, :, column]
+                    for kind in range(1, 3):
+                        total = total + second_in[p, side, kind, :, at].astype(F32)
+                    own_sum[p, :, column] = total
+
     def home_arrived(h):
         c_own(h).wait()
         others(RING, x, lambda peer: c_copy(h, peer, peer).wait_recv())
@@ -601,20 +612,13 @@
             def _(i):
                 put_wide(pl.ds(i * SLAB_ROWS, SLAB_ROWS), home_in[at_index(1, k * few + i, SLOTS)].astype(F32))
 
-            for p in range(2):
-                for side in range(2):
-
-                    @pl.loop(0, PART // 2)
-                    def _(n):
-                        at = pl.ds(pl.multiple_of(n * OUT, OUT), OUT)
-                        column = pl.multiple_of(side * half + n * OUT, OUT)
-                        total = own_sum[p, own, pl.ds(column, OUT)]
-                        for kind in range(1, 3):
-                            total = total + second_in[p, side, kind, own, at].astype(F32)
-                        place = p * PART + side * (PART // 2) + n
-                        total = total + get_wide(pl.ds(place, few, stride=SLAB_ROWS), OUT)
-                        column = pl.multiple_of((2 * p + side) * half + n * OUT, OUT)
-                        out[own, pl.ds(column, OUT)] = total.astype(BF16)
+            @pl.loop(0, SLAB_ROWS)
+            def _(n):
+                column = pl.multiple_of(n * OUT, OUT)
+                at = pl.ds(pl.multiple_of(n % PART * OUT, OUT), OUT)
+                total = own_sum[n // PART, own, at]
+                total = total + get_wide(pl.ds(n, few, stride=SLAB_ROWS), OUT)
+                out[own, pl.ds(column, OUT)] = total.astype(BF16)
 
     def all_left():
         others(CHIPS, chip, lambda peer: x_copy(peer, peer).wait_send())
@@ -629,22 +633,28 @@
     group_start()
     owner_start(0)
     base_arrived()
-    reduce_far(0)
+    reduce_far(0, 0)
+    reduce_far(1, 0)
+    reduce_far(0, 1)
+    reduce_far(1, 1)
+    reduce_near(0, 0)
+    reduce_near(1, 0)
     owner_start(1)
-    reduce_far(1)
-    reduce_near(0)
-    reduce_near(1)
+    reduce_near(0, 1)
+    reduce_near(1, 1)
+    reduce_pass(0, 0)
+    reduce_pass(1, 0)
     latent_part(0)
-    reduce_pass(0)
-    reduce_pass(1)
+    reduce_pass(0, 1)
+    reduce_pass(1, 1)
     latent_part(1)
     back_start(0)
     back_start(1)
     reduce_second(0, 0)
     reduce_second(1, 0)
-    home_start(0)
     reduce_second(0, 1)
     reduce_second(1, 1)
+    home_start(0)
     second_pass(0, 0)
     second_pass(1, 0)
     home_start(1)
@@ -730,7 +740,7 @@
         ),
         name="verify_rows",
     )(
-        draft_row_client.reshape(HOME, 1),
+        draft_row_client.reshape(1, HOME),
         client_rank_bin.reshape(1, tenants),
         client_device.reshape(1, tenants),
         hidden,

time: 193 us -> 191 us (0.990)
  no operation moved by 1% of the time
where the time goes in v6:
time: 191 us; the launch traced here: 189 us
  Pallas kernels  187 us (98%)
  local copies, waits for them, and re-layouts  2.26 us (1%)
    pallas_call x1, Pallas kernels, local(): pl.pallas_call(body, out_shape=(jax.ShapeDtypeStruct((HOME, width), BF16)...  187 us

profile of v6, /device:TPU:0, one launch (start us, length us, event | category | flops | bytes accessed | tf_op | source)
XLA Modules:
  0.0 189.1 jit_solution(3906179874617110037)
XLA Ops:
  0.0 186.9 %verify_rows.1 = (bf16[64,8192]{1,0:T(8,128)(2,1)}, bf16[2,4,256,2048]{3,2,1,0:T(8,128)(2,1)}) custom-call(s32[1,64]{1,0:T(1,128)} %bitcast.7, s32[1,256]{1,0:T(1,128)} %bitcast.5, s32[1,256]{1,0:T(1,128)} %bitcast.6, bf16[64,14784]{1,0:T(8,128)(2,1)} %hidden.1, bf16[462,8192]{1,0:T(8,128)(2,1)} %weight_in.1, bf16[320,14784]{1,0:T(8,128)(2,1)} %bitcast.4, ...), custom_call_target="tpu_custom_call" | custom-call | tf_op jit(solution)/shard_map/verify_rows/pallas_call | solution.py:686
  186.9 2.3 %copy.9 = bf16[64,8192]{1,0:T(8,128)(2,1)} copy(bf16[64,8192]{1,0:T(8,128)(2,1)} %get-tuple-element.6) | data formatting | bytes 2097152

commit v7 on v6

--- a/solution.py
+++ b/solution.py
@@ -521,23 +521,22 @@
         held[...] = (held[...].astype(F32) + second_in[p, side, 0].astype(F32)).astype(BF16)
         s_copy(p, side, 2).start()
 
-    def reduce_second(p, side):
-        came = (4, 3) if side == 0 else (2, 5)
-        stage = []
-        for i, k in enumerate(came):
+    def stage_copy(p, slot):
+        return pltpu.make_async_copy(
+            fin_hbm.at[p, slot], parts.at[p, slot], local_sem.at[16 + 4 * p + slot]
+        )
+
+    def reduce_stage(p, side):
+        for k in (4, 3) if side == 0 else (2, 5):
             r_copy(p, k).wait_recv()
-            slot = side + 2 * i
-            stage.append(
-                pltpu.make_async_copy(
-                    fin_hbm.at[p, slot], parts.at[p, slot], local_sem.at[16 + 4 * p + slot]
-                )
-            )
         for k in (4 + side, 2 + side):
             r_copy(p, k).wait_send()
-        for copy in stage:
-            copy.start()
-        for copy in stage:
-            copy.wait()
+        for i in range(2):
+            stage_copy(p, side + 2 * i).start()
+
+    def reduce_second(p, side):
+        for i in range(2):
+            stage_copy(p, side + 2 * i).wait()
 
         @pl.loop(0, half // TILE)
         def _(n):
@@ -650,8 +649,12 @@
     latent_part(1)
     back_start(0)
     back_start(1)
+    reduce_stage(0, 0)
+    reduce_stage(1, 0)
     reduce_second(0, 0)
+    reduce_stage(0, 1)
     reduce_second(1, 0)
+    reduce_stage(1, 1)
     reduce_second(0, 1)
     reduce_second(1, 1)
     home_start(0)

time: 191 us -> 191 us (level)
  no operation moved by 1% of the time
where the time goes in v7:
time: 191 us; the launch traced here: 189 us
  Pallas kernels  187 us (98%)
  local copies, waits for them, and re-layouts  2.26 us (1%)
    pallas_call x1, Pallas kernels, local(): pl.pallas_call(body, out_shape=(jax.ShapeDtypeStruct((HOME, width), BF16)...  187 us

profile of v7, /device:TPU:0, one launch (start us, length us, event | category | flops | bytes accessed | tf_op | source)
XLA Modules:
  0.0 189.1 jit_solution(12946422923646620118)
XLA Ops:
  0.0 186.9 %verify_rows.1 = (bf16[64,8192]{1,0:T(8,128)(2,1)}, bf16[2,4,256,2048]{3,2,1,0:T(8,128)(2,1)}) custom-call(s32[1,64]{1,0:T(1,128)} %bitcast.7, s32[1,256]{1,0:T(1,128)} %bitcast.5, s32[1,256]{1,0:T(1,128)} %bitcast.6, bf16[64,14784]{1,0:T(8,128)(2,1)} %hidden.1, bf16[462,8192]{1,0:T(8,128)(2,1)} %weight_in.1, bf16[320,14784]{1,0:T(8,128)(2,1)} %bitcast.4, ...), custom_call_target="tpu_custom_call" | custom-call | tf_op jit(solution)/shard_map/verify_rows/pallas_call | solution.py:689
  186.9 2.3 %copy.9 = bf16[64,8192]{1,0:T(8,128)(2,1)} copy(bf16[64,8192]{1,0:T(8,128)(2,1)} %get-tuple-element.6) | data formatting | bytes 2097152
